TPU v7x, 32 devices: a whole 2x2x4 slice. The times are simulated.
32 devices in a mesh: tm: 4 (over x, core), chan: 8 (over z, y).
Axes of the slice: x: 2, y: 2, z: 4, core: 2. Of those that a mesh axis runs over, the one named last changes fastest.
Arguments:
- strain_rate: bfloat16 [512, 12, 16384], P('chan', 'tm'), may hold values from -600 to 600
- fir_taps: bfloat16 [32], replicated, may hold values from -1 to 1
- source_channels: int32 [128], replicated, may hold values from 0 to 511
Outputs:
- correlations: float32 [128, 512, 1024], P(None, ('chan', 'tm'))
Inputs may be any that keep to these rules, and one draw needn't show every extreme that they name: `source_channels`: repeats may occur.
All inputs are finite; a program needn't handle non-finite values.
Results may differ from a plain program's by a relative error of at most 0.0029.
Values may be sent and summed in bfloat16 or wider, within the bound.
No kernel may reach another device: no remote copies, remote signals or barrier semaphores. Data moves between devices by JAX's collectives and lax.ppermute only.
A program may use at most 192 MiB of HBM per device.

v0:
```python
import math

import jax
import jax.numpy as jnp
from jax import lax
from jax.sharding import PartitionSpec as P

WIN = 4096
NFREQ = 512
BANDW = 64
K_LO = 32
LAGS = 1024


def forward_table(length, bins, first_bin):
    sample_index = lax.broadcasted_iota(jnp.int32, (length, bins), 0)
    bin_index = lax.broadcasted_iota(jnp.int32, (length, bins), 1) + first_bin
    phases = sample_index * bin_index % (2 * length)
    angles = phases.astype(jnp.float32) * (math.pi / length)
    return jnp.concatenate([jnp.cos(angles), -jnp.sin(angles)], axis=1)


def lag_table(bins, first_bin, length, lag_count):
    bin_index = lax.broadcasted_iota(jnp.int32, (bins, lag_count), 0) + first_bin
    lag_index = lax.broadcasted_iota(jnp.int32, (bins, lag_count), 1) - lag_count // 2 + 2 * length
    phases = bin_index * lag_index % (2 * length)
    angles = phases.astype(jnp.float32) * (math.pi / length)
    return jnp.concatenate([jnp.cos(angles), -jnp.sin(angles)], axis=0)


def whiten(records, fir_taps, table, bins, band_width):
    channels, windows, samples = records.shape
    length = samples // 4
    signal = records.reshape(channels * windows, 1, samples)
    kernel = fir_taps.reshape(1, 1, -1)
    decimated = lax.conv_general_dilated(
        signal, kernel, (4,), [(fir_taps.shape[0] - 1, 0)], preferred_element_type=jnp.float32
    )
    decimated = decimated.reshape(channels * windows, length)
    spectrum = jnp.dot(
        decimated, table, precision=lax.Precision.HIGHEST, preferred_element_type=jnp.float32
    )
    grouped = spectrum.reshape(channels * windows, 2, bins // band_width, band_width)
    band_power = jnp.sum(grouped * grouped, axis=(1, 3), keepdims=True) / band_width
    whitened = grouped * lax.rsqrt(band_power + 1e-06)
    return whitened.reshape(channels, windows, 2, bins).astype(jnp.bfloat16)


def cross_spectra(source_part, local_part):
    src_real = source_part[:, :, 0]
    src_imag = source_part[:, :, 1]
    loc_real = local_part[:, :, 0]
    loc_imag = local_part[:, :, 1]
    pattern = "swk,cwk->sck"
    real_part = jnp.einsum(
        pattern, src_real, loc_real, preferred_element_type=jnp.float32
    ) + jnp.einsum(pattern, src_imag, loc_imag, preferred_element_type=jnp.float32)
    imag_part = jnp.einsum(
        pattern, src_imag, loc_real, preferred_element_type=jnp.float32
    ) - jnp.einsum(pattern, src_real, loc_imag, preferred_element_type=jnp.float32)
    return jnp.stack([real_part, imag_part], axis=2)


def correlate(cross_spec, table, window_total):
    sources, channels, _, bins = cross_spec.shape
    flattened = cross_spec.reshape(sources * channels, 2 * bins)
    result = jnp.dot(
        flattened, table, precision=lax.Precision.HIGHEST, preferred_element_type=jnp.float32
    )
    result = result * (1.0 / math.sqrt(bins * window_total))
    return result.reshape(sources, channels, table.shape[1])


def pick_sources(source_channels, spectra, first_channel):
    channels = spectra.shape[0]
    channel_ids = first_channel + lax.broadcasted_iota(jnp.int32, (1, channels), 1)
    selector = (source_channels[:, None] == channel_ids).astype(jnp.bfloat16)
    flattened = spectra.reshape(channels, -1)
    picked = jnp.dot(selector, flattened, preferred_element_type=jnp.float32)
    return picked.reshape((source_channels.shape[0],) + spectra.shape[1:])


def on_device(strain_rate, fir_taps, source_channels):
    ftable = forward_table(WIN, NFREQ, K_LO)
    spectra = whiten(strain_rate, fir_taps, ftable, NFREQ, BANDW)
    channels = spectra.shape[0]
    windows = spectra.shape[1]
    tm_count = lax.axis_size("tm")
    selection = pick_sources(source_channels, spectra, lax.axis_index("chan") * channels)
    ltable = lag_table(NFREQ, K_LO, WIN, LAGS)
    regrouped = lax.all_to_all(spectra, "tm", split_axis=0, concat_axis=1, tiled=True)
    collected = lax.all_gather(selection.astype(jnp.bfloat16), "tm", axis=1, tiled=True)
    source_part = lax.psum(collected.astype(jnp.float32).astype(jnp.bfloat16), "chan")
    cross_spec = cross_spectra(source_part, regrouped)
    return correlate(cross_spec, ltable, windows * tm_count)


def solution(mesh):
    placed = (P("chan", "tm", None), P(), P())
    return jax.shard_map(
        on_device,
        mesh=mesh,
        in_specs=placed,
        out_specs=P(None, ("chan", "tm"), None),
        check_vma=False,
    )
```

profile of v0, /device:TPU:0, one launch (start us, length us, event | category | flops | bytes accessed | tf_op | source)
XLA Modules:
  0.0 450.3 jit_solution(16884698430919690734)
XLA Ops:
  7.1 36.9 %fusion.9 = (f32[4096,512]{0,1:T(8,128)}, f32[4096,512]{0,1:T(8,128)}) fusion(s32[512]{0:T(512)S(1)} %iota_add_fusion.1), kind=kLoop, calls=%fused_computation.18 | loop fusion | flops 31457280 | bytes 16779264 | tf_op jit(solution)/shard_map/cos | solution.py:20
  44.0 11.4 %copy.26 = bf16[64,3,16384]{2,1,0:T(4,128)(2,1)} copy(bf16[64,3,16384]{2,0,1:T(8,128)(2,1)} %param.3) | data formatting | bytes 12582912 | tf_op args[0]
  55.4 10.2 %reshape.38 = bf16[192,1,16384]{2,0,1:T(8,128)(2,1)} reshape(bf16[64,3,16384]{2,1,0:T(4,128)(2,1)} %copy.26) | data formatting | bytes 12582912 | tf_op jit(solution)/shard_map/reshape | solution.py:34
  65.6 34.0 %copy.27 = bf16[192,1,16384]{0,1,2:T(2,128)(2,1)} copy(bf16[192,1,16384]{2,0,1:T(8,128)(2,1)} %reshape.38) | data formatting | bytes 12582912 | tf_op jit(solution)/shard_map/reshape | solution.py:34
  99.8 56.7 %fusion.29 = f32[192,1,4096]{0,1,2:T(1,128)} fusion(bf16[192,1,16384]{0,1,2:T(2,128)(2,1)} %copy.27, bf16[1,1,32]{1,0,2:T(2,128)(2,1)S(1)} %copy.28), kind=kOutput, calls=%fused_computation.53 | convolution fusion | flops 50279424 | bytes 9437248 | tf_op jit(solution)/shard_map/conv_general_dilated | solution.py:36
  156.5 9.3 %copy.29 = f32[192,1,4096]{2,0,1:T(8,128)S(1)} copy(f32[192,1,4096]{0,1,2:T(1,128)} %fusion.29) | data formatting | bytes 6291456 | tf_op jit(solution)/shard_map/conv_general_dilated | solution.py:36
  165.8 7.0 %pad_maximum_fusion = f32[4096,1024]{0,1:T(8,128)S(1)} fusion(f32[4096,512]{0,1:T(8,128)} %get-tuple-element.10, f32[4096,512]{0,1:T(8,128)} %get-tuple-element.9), kind=kLoop, calls=%fused_computation | loop fusion | flops 4194304 | bytes 33554432 | tf_op jit(solution)/shard_map/concatenate | solution.py:20
  172.8 14.2 %multiply_reduce_fusion = (f32[192,8]{0,1:T(8,128)S(1)}, f32[192,2,8,64]{0,3,2,1:T(8,128)S(1)}) fusion(f32[2,8,64,4096]{3,2,1,0:T(8,128)S(1)} %bitcast.63, f32[192,1,4096]{2,0,1:T(8,128)S(1)} %copy.29), kind=kOutput, calls=%fused_computation.41 | convolution fusion | flops 9664067584 | bytes 20715520 | tf_op jit(solution)/shard_map/dot_general | solution.py:40
  188.6 1.4 convolution_convert_fusion
  190.1 31.3 %all-gather.2.cloned.1.call-done = bf16[128,12,2,512]{3,0,2,1:T(8,128)(2,1)} async-done(((bf16[128,3,2,512]{3,0,2,1:T(8,128)(2,1)}), bf16[128,12,2,512]{3,0,2,1:T(8,128)(2,1)}) %all-gather.2.cloned.1.call-update) | async-done | bytes 3145744 | tf_op jit(solution)/shard_map/all_gather | solution.py:92
  221.4 7.9 %copy.35 = bf16[128,12,2,512]{0,1,3,2:T(8,128)(2,1)} copy(bf16[128,12,2,512]{3,0,2,1:T(8,128)(2,1)} %all-gather.2.cloned.1.call-done) | data formatting | bytes 6291456 | tf_op jit(solution)/shard_map/all_gather | solution.py:92
  230.5 3.5 all-to-all-start
  234.0 9.8 %fusion.21 = (f32[512,1024]{1,0:T(8,128)}, f32[512,1024]{1,0:T(8,128)}) fusion(s32[1024]{0:T(1024)S(1)} %iota_add_fusion, s32[512]{0:T(512)S(1)} %copy-done.5), kind=kLoop, calls=%fused_computation.39 | loop fusion | flops 7864320 | bytes 4200448 | tf_op jit(solution)/shard_map/cos | solution.py:28
  243.9 3.0 copy.40
  246.8 2.1 copy.41
  249.0 136.8 %all-reduce.2.cloned.1.call-done = bf16[128,12,2,512]{0,1,3,2:T(8,128)(2,1)} async-done(((bf16[128,12,2,512]{0,1,3,2:T(8,128)(2,1)}), bf16[128,12,2,512]{0,1,3,2:T(8,128)(2,1)}) %all-reduce.2.cloned.1.call-update) | async-done | bytes 3145744 | tf_op jit(solution)/shard_map/psum | solution.py:93
  385.8 3.6 fusion.19
  389.9 1.2 fusion.17
  391.1 1.2 add_bitcast_fusion
  392.3 1.2 subtract_bitcast_fusion
  393.5 3.9 pad_maximum_fusion.1
  397.5 10.6 %copy.37 = f32[128,16,2,512]{3,2,1,0:T(2,128)} copy(f32[128,16,2,512]{0,1,3,2:T(8,128)} %pad_maximum_fusion.1) | data formatting | bytes 16777216 | tf_op jit(solution)/shard_map/stack | solution.py:61
  408.1 5.6 %copy.42 = f32[256,8,2,512]{3,1,2,0:T(8,128)S(1)} copy(f32[256,8,2,512]{3,2,1,0:T(2,128)} %bitcast.64) | data formatting | bytes 16777216
  413.8 29.3 %convolution_multiply_fusion = f32[2048,1024]{1,0:T(8,128)} fusion(f32[2048,1024]{1,0:T(8,128)S(1)} %bitcast.65, f32[512,1024]{1,0:T(8,128)S(1)} %copy-done.3, f32[512,1024]{1,0:T(8,128)S(1)} %copy-done.2), kind=kOutput, calls=%fused_computation.12 | convolution fusion | flops 25772949504 | bytes 20971520 | tf_op jit(solution)/shard_map/dot_general | solution.py:67
  (33 shorter events, 4.1 us)
Async XLA Ops:
  6.5 214.9 %all-gather.2.cloned.1.call-start = ((), (), s32[]{:S(2)}) async-start(), calls=%async_computation.1 | async-start | bytes 3932160 | tf_op jit(solution)/shard_map/all_gather | solution.py:92
  6.5 0.6 copy-start.4
  65.6 34.0 %copy-start.7 = (bf16[32]{0:T(256)(128)(2,1)S(1)}, bf16[32]{0:T(256)(128)(2,1)}, u32[]{:S(2)}) copy-start(bf16[32]{0:T(256)(128)(2,1)} %param.4) | copy-start | bytes 196
  187.0 1.6 copy-start.6
  190.0 195.8 %all-reduce.2.cloned.1.call-start = ((), (), s32[]{:S(2)}) async-start(), calls=%async_computation.2 | async-start | bytes 8388608 | tf_op jit(solution)/shard_map/psum | solution.py:93
  229.3 4.7 %copy-start.5 = (s32[512]{0:T(512)S(1)}, s32[512]{0:T(512)}, u32[]{:S(2)}) copy-start(s32[512]{0:T(512)} %copy-done.4) | copy-start | bytes 6148
  230.5 13.3 %all-to-all-start = ((bf16[64,3,2,512]{3,2,1,0:T(2,128)(2,1)}), bf16[64,3,2,512]{3,2,1,0:T(2,128)(2,1)S(1)}, u32[]{:S(2)}, u32[]{:S(2)}) async-start(bf16[64,3,2,512]{3,2,1,0:T(2,128)(2,1)} %convert_element_type.28), calls=%async_computation | async-start | bytes 786432 | tf_op jit(solution)/shard_map/all_to_all | solution.py:91
  385.8 3.6 copy-start
  385.8 4.1 copy-start.1
  408.1 5.7 %copy-start.2 = (f32[512,1024]{1,0:T(8,128)S(1)}, f32[512,1024]{1,0:T(8,128)}, u32[]{:S(2)}) copy-start(f32[512,1024]{1,0:T(8,128)} %get-tuple-element.7) | copy-start | bytes 6291460
  408.1 5.7 %copy-start.3 = (f32[512,1024]{1,0:T(8,128)S(1)}, f32[512,1024]{1,0:T(8,128)}, u32[]{:S(2)}) copy-start(f32[512,1024]{1,0:T(8,128)} %get-tuple-element.8) | copy-start | bytes 6291460
Sparse Core Ops, SparseCore 0:
  190.1 31.2 all-gather.1
  229.4 156.2 all-reduce.1
where the time goes:
time: 458 us; the launch traced here: 450 us
  waiting for transfers between devices  168 us (37%)
  matrix products  109 us (24%)
  local copies, waits for them, and re-layouts  98.2 us (21%)
  other arithmetic  57.7 us (13%)
  between operations  14 us (3%)
    psum x1, waiting for transfers between devices, on_device(): lax.psum(collected.astype(jnp.float32).astype(jnp.bfloat16), 'chan')  137 us
    conv_general_dilated x1, matrix products, whiten(): lax.conv_general_dilated(signal, kernel, (4,), [(fir_taps.shape[0] - 1, 0...  56.7 us
    reshape x2, local copies, waits for them, and re-layouts, whiten(): signal = records.reshape(channels * windows, 1, samples)  44.3 us
    cos x1, other arithmetic, forward_table(): return jnp.concatenate([jnp.cos(angles), -jnp.sin(angles)], axis=1)  36.9 us
    all_gather x1, waiting for transfers between devices, on_device(): lax.all_gather(selection.astype(jnp.bfloat16), 'tm', axis=1, tiled=True)  31.3 us
    dot_general x1, matrix products, correlate(): jnp.dot(flattened, table, precision=lax.Precision.HIGHEST, preferred_elem...  29.3 us
    unnamed x20, local copies, waits for them, and re-layouts  23.2 us
    dot_general x1, matrix products, whiten(): jnp.dot(decimated, table, precision=lax.Precision.HIGHEST, preferred_elem...  14.2 us
  transfers between devices with their start and end apart: 3, of which 2 were waited for; matrix products, arithmetic and copies ran while one was open for 4% of the time, Pallas kernels for 0%

commit v1 on v0

v1 whole, which is shorter than its diff:
```python
import functools
import math

import jax
import jax.numpy as jnp
import numpy as np
from jax import lax
from jax.experimental import pallas as pl
from jax.experimental.pallas import tpu as pltpu
from jax.sharding import PartitionSpec as P

WIN = 4096
NFREQ = 512
BANDW = 64
K_LO = 32
LAGS = 1024
TAPS = 32
SUB = 512
GROUP = 8
SPEC = 2 * NFREQ
FIR_OUT = 256
FIR_IN = 4 * FIR_OUT + 128
MIB = 1 << 20


def forward_constants():
    samples = np.arange(SUB)[:, None]
    bins = np.arange(NFREQ)[None, :] + K_LO
    angles = 2.0 * np.pi * ((samples * bins) % (2 * WIN)) / (2 * WIN)
    table = np.concatenate([np.cos(angles), -np.sin(angles)], axis=1)
    high = table.astype(jnp.bfloat16)
    low = (table - high.astype(np.float64)).astype(jnp.bfloat16)
    return np.concatenate([high, high, low], axis=0)


def lag_constant():
    group, part, inner = np.meshgrid(
        np.arange(NFREQ // GROUP), np.arange(2), np.arange(GROUP), indexing="ij"
    )
    bins = (group * GROUP + inner).reshape(-1, 1) + K_LO
    lags = np.arange(LAGS)[None, :] - LAGS // 2 + 2 * WIN
    angles = 2.0 * np.pi * ((bins * lags) % (2 * WIN)) / (2 * WIN)
    table = np.where(part.reshape(-1, 1) == 0, np.cos(angles), -np.sin(angles))
    return table.astype(jnp.bfloat16)


def dot(a, b):
    return jnp.dot(a, b, preferred_element_type=jnp.float32)


def dot_nt(a, b):
    return lax.dot_general(a, b, (((1,), (1,)), ((), ())), preferred_element_type=jnp.float32)


def dot_tn(a, b):
    return lax.dot_general(a, b, (((0,), (0,)), ((), ())), preferred_element_type=jnp.float32)


def split(x):
    high = x.astype(jnp.bfloat16)
    return high, (x - high.astype(jnp.float32)).astype(jnp.bfloat16)


def turn_values(shape):
    index = (lax.broadcasted_iota(jnp.int32, shape, 1) + K_LO) % 16
    real = jnp.zeros(shape, jnp.float32)
    imag = jnp.zeros(shape, jnp.float32)
    for i in range(16):
        real = jnp.where(index == i, math.cos(math.pi * i / 8), real)
        imag = jnp.where(index == i, -math.sin(math.pi * i / 8), imag)
    return real, imag


def factors(chan_count, tm_count):
    inner = 2 if chan_count <= 8 else 4
    return {"z": chan_count // inner, "y": inner, "x": tm_count // 2, "c": 2}


def moved(sizes, index, outer, inner, by_outer, by_inner):
    n_outer, n_inner = sizes[outer], sizes[inner]
    hi = lax.rem(lax.div(index, n_inner) + by_outer + n_outer, n_outer)
    lo = lax.rem(lax.rem(index, n_inner) + by_inner + n_inner, n_inner)
    return hi * n_inner + lo


def chan_at(sizes, by_z, by_y):
    return moved(sizes, lax.axis_index("chan"), "z", "y", by_z, by_y)


def tm_at(sizes, by_x, by_c):
    return moved(sizes, lax.axis_index("tm"), "x", "c", by_x, by_c)


def shifted(sizes, value, **by):
    if not any(by.values()):
        return value
    axis, outer, inner = ("chan", "z", "y") if set(by) <= {"z", "y"} else ("tm", "x", "c")
    n_outer, n_inner = sizes[outer], sizes[inner]
    pairs = []
    for index in range(n_outer * n_inner):
        hi = (index // n_inner + by.get(outer, 0)) % n_outer
        lo = (index % n_inner + by.get(inner, 0)) % n_inner
        pairs.append((index, hi * n_inner + lo))
    return lax.ppermute(value, axis, pairs)


def fir_kernel(x_hbm, fir_hbm, out_ref, x_ref, fir_ref, toeplitz, sems, *, windows):
    chans = x_ref.shape[0] // windows
    fetch_fir = pltpu.make_async_copy(fir_hbm, fir_ref, sems.at[windows])
    fetch_fir.start()
    fetches = []
    for w in range(windows):
        mine = pl.ds(w * chans, chans)
        fetches.append(pltpu.make_async_copy(x_hbm.at[mine], x_ref.at[mine], sems.at[w]))
        fetches[-1].start()
    in_index = lax.broadcasted_iota(jnp.int32, (256, 128), 0)
    out_index = lax.broadcasted_iota(jnp.int32, (256, 128), 1)
    tap = in_index - 4 * (out_index % TAPS) - 97
    small = jnp.zeros((256, 128), jnp.float32)
    fetch_fir.wait()
    taps = fir_ref[...].astype(jnp.float32)
    for j in range(TAPS):
        small = jnp.where(tap == j, taps[0:1, j : j + 1], small)
    slot = lax.broadcasted_iota(jnp.int32, (128, 128), 1) // TAPS
    for a in range(FIR_IN // 128):
        for n in range(FIR_OUT // 128):
            here = jnp.where(slot + n * (128 // TAPS) == a, small[:128], 0.0)
            here = jnp.where(slot + n * (128 // TAPS) == a - 1, small[128:], here)
            toeplitz[a * 128 : (a + 1) * 128, n * 128 : (n + 1) * 128] = here.astype(jnp.bfloat16)

    step = 4 * FIR_OUT
    per = SUB // FIR_OUT
    together = 4

    def work(pieces, mine, first):
        piece = dot(jnp.concatenate(pieces, axis=0), toeplitz[...])
        high, low = split(piece)
        for n in range(together):
            i = (first + n) // per
            at = (n % per) * FIR_OUT
            part = slice(n * chans, (n + 1) * chans)
            out_ref[i, mine, at : at + FIR_OUT] = high[part]
            out_ref[i, mine, SUB + at : SUB + at + FIR_OUT] = low[part]
            out_ref[i, mine, 2 * SUB + at : 2 * SUB + at + FIR_OUT] = high[part]

    for w in range(windows):
        mine = slice(w * chans, (w + 1) * chans)
        fetches[w].wait()
        pieces = [jnp.concatenate([jnp.zeros((chans, 128), jnp.bfloat16), x_ref[mine, :step]], axis=1)]
        for n in range(1, together):
            pieces.append(x_ref[mine, n * step - 128 : (n + 1) * step])
        work(pieces, mine, 0)

        def body(j, carry, mine=mine):
            pieces = []
            for n in range(together):
                first = pl.multiple_of((j * together + n) * step - 128, 128)
                pieces.append(x_ref[mine, pl.ds(first, step + 128)])
            work(pieces, mine, j * together)
            return carry

        lax.fori_loop(1, WIN // FIR_OUT // together, body, 0)


def whiten_kernel(part_ref, *refs, windows, sizes):
    tm_count = sizes["x"] * sizes["c"]
    bins_out = refs[: sizes["z"]]
    rows_out = refs[sizes["z"] : sizes["z"] + tm_count]
    bins_ref, rows_ref = refs[sizes["z"] + tm_count :]
    blocks, rows, _ = part_ref.shape
    chans = rows // windows
    width = bins_ref.shape[2]
    own = rows_ref.shape[2]
    quarters = NFREQ // 128
    turn_re, turn_im = turn_values((1, NFREQ))
    band_a = lax.broadcasted_iota(jnp.int32, (128, 128), 0) // BANDW
    band_b = lax.broadcasted_iota(jnp.int32, (128, 128), 1) // BANDW
    same_band = (band_a == band_b).astype(jnp.bfloat16)
    src = lax.broadcasted_iota(jnp.int32, (256, 256), 0)
    dst = lax.broadcasted_iota(jnp.int32, (256, 256), 1)
    wanted = (dst // (2 * GROUP)) * GROUP + dst % GROUP + 128 * ((dst // GROUP) % 2)
    order = (src == wanted).astype(jnp.bfloat16)
    for w in range(windows):
        mine = slice(w * chans, (w + 1) * chans)
        real = part_ref[blocks - 1, mine, :NFREQ]
        imag = part_ref[blocks - 1, mine, NFREQ:]
        for i in reversed(range(blocks - 1)):
            real, imag = (
                part_ref[i, mine, :NFREQ] + real * turn_re - imag * turn_im,
                part_ref[i, mine, NFREQ:] + real * turn_im + imag * turn_re,
            )
        re = jnp.concatenate([real[:, q * 128 : (q + 1) * 128] for q in range(quarters)], axis=0)
        im = jnp.concatenate([imag[:, q * 128 : (q + 1) * 128] for q in range(quarters)], axis=0)
        power = re * re + im * im
        p0, p1 = split(power)
        p2 = (power - p0.astype(jnp.float32) - p1.astype(jnp.float32)).astype(jnp.bfloat16)
        total = dot(jnp.concatenate([p0, p1, p2], axis=1), jnp.concatenate([same_band] * 3, axis=0))
        gain = lax.rsqrt(total * (1.0 / BANDW) + 1e-06)
        both = jnp.concatenate(
            [(re * gain).astype(jnp.bfloat16), (im * gain).astype(jnp.bfloat16)], axis=1
        )
        both = dot(both, order).astype(jnp.bfloat16)
        for q in range(quarters):
            part = both[q * chans : (q + 1) * chans]
            for n in range(max(1, 256 // width)):
                bins_ref[q * 256 // width + n, mine] = part[:, n * width : (n + 1) * width]
            for t in range(tm_count):
                rows_ref[t, w, :, q * 256 : (q + 1) * 256] = part[t * own : (t + 1) * own]
    for z in range(sizes["z"]):
        for y in range(sizes["y"]):
            bins_out[z][y] = bins_ref[chan_at(sizes, z, y)]
    for x in range(sizes["x"]):
        for c in range(sizes["c"]):
            rows_out[x * sizes["c"] + c][...] = rows_ref[tm_at(sizes, x, c)]


def whitened_spectra(strain, taps, sizes):
    chans, windows, samples = strain.shape
    rows = chans * windows
    chan_count = sizes["z"] * sizes["y"]
    tm_count = sizes["x"] * sizes["c"]
    width = SPEC // chan_count
    own = chans // tm_count
    x = jnp.transpose(strain, (1, 0, 2)).reshape(rows, samples)
    blocks = WIN // SUB
    filtered = pl.pallas_call(
        functools.partial(fir_kernel, windows=windows),
        in_specs=[pl.BlockSpec(memory_space=pl.ANY)] * 2,
        out_shape=jax.ShapeDtypeStruct((blocks, rows, 3 * SUB), jnp.bfloat16),
        scratch_shapes=[
            pltpu.VMEM((rows, samples), jnp.bfloat16),
            pltpu.VMEM((1, TAPS), jnp.bfloat16),
            pltpu.VMEM((FIR_IN, FIR_OUT), jnp.bfloat16),
            pltpu.SemaphoreType.DMA((windows + 1,)),
        ],
        compiler_params=pltpu.CompilerParams(vmem_limit_bytes=58 * MIB),
        name="fir",
    )(x, taps.reshape(1, TAPS))
    part = dot(filtered.reshape(blocks * rows, 3 * SUB), jnp.asarray(forward_constants()))
    outs = pl.pallas_call(
        functools.partial(whiten_kernel, windows=windows, sizes=sizes),
        out_shape=[jax.ShapeDtypeStruct((sizes["y"], rows, width), jnp.bfloat16)] * sizes["z"]
        + [jax.ShapeDtypeStruct((windows, own, SPEC), jnp.bfloat16)] * tm_count,
        scratch_shapes=[
            pltpu.VMEM((chan_count, rows, width), jnp.bfloat16),
            pltpu.VMEM((tm_count, windows, own, SPEC), jnp.bfloat16),
        ],
        compiler_params=pltpu.CompilerParams(vmem_limit_bytes=24 * MIB),
        name="whiten",
    )(part.reshape(blocks, rows, SPEC))
    return outs[: sizes["z"]], outs[sizes["z"] :]


def pick_kernel(channels_ref, *refs, windows, sizes):
    bins = refs[: sizes["z"]]
    outs = refs[sizes["z"] :]
    chans = bins[0].shape[1] // windows
    sources = channels_ref.shape[1]
    chosen = []
    for z in range(sizes["z"]):
        first = chan_at(sizes, -z, 0) * chans
        ids = lax.broadcasted_iota(jnp.int32, (chans, sources), 0) + first
        chosen.append((ids == channels_ref[...]).astype(jnp.bfloat16))
    chosen = jnp.concatenate(chosen, axis=0)
    for y in range(sizes["y"]):
        for w in range(windows):
            block = jnp.concatenate([b[y, w * chans : (w + 1) * chans, :] for b in bins], axis=0)
            outs[y][0, w] = dot_tn(block, chosen).astype(jnp.bfloat16)


def picked_sources(source_channels, bins, windows, sizes):
    sources = source_channels.shape[0]
    width = bins[0].shape[2]
    shape = (1, windows, width, sources)
    parts = pl.pallas_call(
        functools.partial(pick_kernel, windows=windows, sizes=sizes),
        out_shape=[jax.ShapeDtypeStruct(shape, jnp.bfloat16)] * sizes["y"],
        compiler_params=pltpu.CompilerParams(vmem_limit_bytes=16 * MIB),
        name="pick",
    )(source_channels.reshape(1, sources), *bins)
    total = parts[0]
    for y in range(1, sizes["y"]):
        total = total + shifted(sizes, parts[y], y=y)
    return total


def block_at(sizes, step, sign):
    if sizes is None:
        return step
    z = lax.div(step, sizes["y"])
    y = lax.rem(step, sizes["y"])
    return chan_at(sizes, sign * z, sign * y)


def expand_kernel(*refs, sizes):
    out_ref = refs[-1]
    windows, own, _ = refs[0].shape
    depth = windows * (len(refs) - 1) * 2 * GROUP
    groups = 128 // (2 * GROUP)
    lane = lax.broadcasted_iota(jnp.int32, (own, 128), 1)
    first = lane % (2 * GROUP) < GROUP
    bin_row = lax.broadcasted_iota(jnp.int32, (own, GROUP, depth), 1)
    bin_lane = lax.broadcasted_iota(jnp.int32, (own, GROUP, depth), 2) % GROUP
    same = bin_row == bin_lane

    def body(step, carry):
        lanes = pl.ds(pl.multiple_of(block_at(sizes, step, -1) * 128, 128), 128)
        plain = []
        swapped = []
        for ref in refs[:-1]:
            for w in range(windows):
                x = ref[w, :, lanes].astype(jnp.float32)
                plain.append(x)
                ahead = pltpu.roll(x, 128 - GROUP, 1)
                behind = pltpu.roll(x, GROUP, 1)
                swapped.append(jnp.where(first, -ahead, behind))
        for g in range(groups):
            at = slice(g * 2 * GROUP, (g + 1) * 2 * GROUP)
            for p, parts in enumerate((plain, swapped)):
                a = jnp.concatenate([x[:, at] for x in parts], axis=1)
                full = jnp.where(same, a[:, None, :], 0.0)
                out_ref[step * groups + g, :, p * GROUP : (p + 1) * GROUP, :] = full.astype(jnp.bfloat16)
        return carry

    lax.fori_loop(0, SPEC // 128, body, 0)


def expanded_local(local, sizes):
    windows, own, _ = local[0].shape
    depth = windows * len(local) * 2 * GROUP
    out = pl.pallas_call(
        functools.partial(expand_kernel, sizes=sizes),
        out_shape=jax.ShapeDtypeStruct((SPEC // (2 * GROUP), own, 2 * GROUP, depth), jnp.bfloat16),
        cost_estimate=pl.CostEstimate(flops=4 * 10**9, bytes_accessed=8 * MIB, transcendentals=0),
        compiler_params=pltpu.CompilerParams(vmem_limit_bytes=24 * MIB),
        name="expand",
    )(*local)
    return out.reshape(SPEC // (2 * GROUP), own * 2 * GROUP, depth)


def cross_kernel(local_ref, *refs, fetch, own, sizes, by_y, aliased):
    sources = refs[: len(refs) - 2 - aliased]
    out_ref, wide = refs[-2:]
    count = sources[0].shape[-1]
    groups = 128 // (2 * GROUP)
    row = lax.broadcasted_iota(jnp.int32, (count, count), 0)
    column = lax.broadcasted_iota(jnp.int32, (count, count), 1)
    identity = (row == column).astype(jnp.bfloat16)

    def body(index, carry):
        step = index if by_y is None else index * sizes["y"] + by_y
        tiles = fetch(sources, step)
        cross = []
        for g in range(groups):
            rows = slice(g * 2 * GROUP, (g + 1) * 2 * GROUP)
            block = jnp.concatenate([tile[rows] for tile in tiles], axis=0)
            cross.append(dot(local_ref[step * groups + g], block).astype(jnp.bfloat16))
        tall = jnp.concatenate(
            [x[c * 2 * GROUP : (c + 1) * 2 * GROUP] for c in range(own) for x in cross], axis=0
        )
        turned = dot_nt(identity, tall)
        for c in range(own):
            wide[pl.ds(c, count, stride=own), :] = turned[:, c * 128 : (c + 1) * 128]
        lanes = pl.ds(pl.multiple_of(block_at(sizes, step, -1) * 128, 128), 128)
        out_ref[:, lanes] = wide[...].astype(jnp.bfloat16)
        return carry

    lax.fori_loop(0, SPEC // 128 if by_y is None else sizes["z"], body, 0)


def crossed(local, sources, fetch, sizes, by_y=None, held=None):
    _, expanded_rows, _ = local.shape
    own = expanded_rows // (2 * GROUP)
    count = sources[0].shape[-1]
    shape = jax.ShapeDtypeStruct((count * own, SPEC), jnp.bfloat16)
    extra = [] if held is None else [held]
    specs = [pl.BlockSpec(memory_space=pltpu.VMEM)] * (1 + len(sources))
    return pl.pallas_call(
        functools.partial(
            cross_kernel, fetch=fetch, own=own, sizes=sizes, by_y=by_y, aliased=len(extra)
        ),
        in_specs=specs + [pl.BlockSpec(memory_space=pltpu.VMEM)] * len(extra),
        out_shape=shape,
        input_output_aliases={1 + len(sources): 0} if extra else {},
        scratch_shapes=[pltpu.VMEM((count * own, 128), jnp.float32)],
        cost_estimate=pl.CostEstimate(flops=4 * 10**9, bytes_accessed=8 * MIB, transcendentals=0),
        compiler_params=pltpu.CompilerParams(vmem_limit_bytes=32 * MIB),
        name="cross",
    )(local, *sources, *extra)


def lag_kernel(cross_ref, table_ref, out_hbm, buffer, sems, *, scale):
    depth, height, lags = buffer.shape
    steps = cross_ref.shape[0] // height

    def store(i):
        mine = pl.ds(pl.multiple_of(i * height, height), height)
        slot = lax.rem(i, depth)
        return pltpu.make_async_copy(buffer.at[slot], out_hbm.at[mine], sems.at[slot])

    def body(i, carry):
        @pl.when(i >= depth)
        def _():
            store(i - depth).wait()

        rows = cross_ref[pl.ds(pl.multiple_of(i * height, height), height)]
        slot = lax.rem(i, depth)
        for n in range(lags // 256):
            at = slice(n * 256, (n + 1) * 256)
            buffer[slot, :, at] = dot(rows, table_ref[:, at]) * scale
        store(i).start()
        return carry

    lax.fori_loop(0, steps, body, 0)
    for i in range(max(0, steps - depth), steps):
        store(i).wait()


def correlations(cross, source_count, window_total):
    rows = cross.shape[0]
    height = 512
    out = pl.pallas_call(
        functools.partial(lag_kernel, scale=1.0 / math.sqrt(NFREQ * window_total)),
        in_specs=[pl.BlockSpec(memory_space=pltpu.VMEM)] * 2,
        out_specs=pl.BlockSpec(memory_space=pl.ANY),
        out_shape=jax.ShapeDtypeStruct((rows, LAGS), jnp.float32),
        scratch_shapes=[
            pltpu.VMEM((2, height, LAGS), jnp.float32),
            pltpu.SemaphoreType.DMA((2,)),
        ],
        compiler_params=pltpu.CompilerParams(vmem_limit_bytes=24 * MIB),
        name="lags",
    )(cross, jnp.asarray(lag_constant()))
    return out.reshape(source_count, -1, LAGS)


def gathered(picked, local, sizes):
    windows, width = picked.shape[1:3]
    half = width // 2
    whole = jnp.concatenate([shifted(sizes, picked, z=d) for d in range(sizes["z"])], axis=0)
    held = {(0, 0): [whole]}
    for x in range(1, sizes["x"]):
        held[x, 0] = [shifted(sizes, whole, x=x)]
    for y in range(1, sizes["y"]):
        held[0, y] = [shifted(sizes, whole, y=y)]
    expanded = expanded_local(local, sizes)
    edges = {key: array for key, array in held.items() if key != (0, 0)}
    edges, expanded = lax.optimization_barrier((edges, expanded))
    held.update(edges)
    for x in range(1, sizes["x"]):
        for y in range(1, sizes["y"]):
            held[x, y] = [
                shifted(sizes, held[0, y][0][:, :, :half], x=x),
                shifted(sizes, held[x, 0][0][:, :, half:], y=y),
            ]

    def rows_of(y):
        arrays = []
        place = {}
        for x in range(sizes["x"]):
            for c in range(sizes["c"]):
                place[x, c] = len(arrays)
                arrays += [shifted(sizes, array, c=c) for array in held[x, y]]

        def fetch(refs, step):
            by_z = lax.div(step, sizes["y"])
            tiles = []
            for x in range(sizes["x"]):
                for c in range(sizes["c"]):
                    parts = refs[place[x, c] : place[x, c] + len(held[x, y])]
                    for w in range(windows):
                        tiles.append(jnp.concatenate([part[by_z, w] for part in parts], axis=0))
            return tiles

        return arrays, fetch

    cross = None
    for y in range(sizes["y"]):
        if y > 0:
            far = {key: array for key, array in held.items() if key[0] and key[1]}
            far, cross = lax.optimization_barrier((far, cross))
            held.update(far)
        arrays, fetch = rows_of(y)
        cross = crossed(expanded, arrays, fetch, sizes, by_y=y, held=cross)
    return cross


def gathered_plainly(picked, local, sizes):
    parts = [shifted(sizes, picked, x=x, c=c) for x in range(sizes["x"]) for c in range(sizes["c"])]
    mine = jnp.concatenate(parts, axis=1)[0]
    total, width, count = mine.shape
    held = lax.all_gather(mine, "chan", axis=0, tiled=False)
    held = held.reshape(SPEC // 128, 128 // width, total, width, count)
    held = jnp.transpose(held, (0, 2, 1, 3, 4)).reshape(SPEC // 128, total, 128, count)

    def fetch(refs, step):
        return [refs[0][step, i] for i in range(total)]

    return crossed(expanded_local(local, None), [held], fetch, None)


def on_device(strain_rate, fir_taps, source_channels):
    sizes = factors(lax.axis_size("chan"), lax.axis_size("tm"))
    windows = strain_rate.shape[1]
    bins, rows = whitened_spectra(strain_rate, fir_taps, sizes)
    bins = [shifted(sizes, b, z=z) for z, b in enumerate(bins)]
    moves = [(x, c) for x in range(sizes["x"]) for c in range(sizes["c"])]
    local = [shifted(sizes, r, x=x, c=c) for r, (x, c) in zip(rows, moves)]
    bins, local = lax.optimization_barrier((bins, local))
    picked = picked_sources(source_channels, bins, windows, sizes)
    gather = gathered if picked.shape[2] == 128 else gathered_plainly
    cross = gather(picked, local, sizes)
    return correlations(cross, source_channels.shape[0], windows * lax.axis_size("tm"))


def solution(mesh):
    placed = (P("chan", "tm", None), P(), P())
    return jax.shard_map(
        on_device,
        mesh=mesh,
        in_specs=placed,
        out_specs=P(None, ("chan", "tm"), None),
        check_vma=False,
    )
```

time: 458 us -> 78.4 us (0.17); the launches traced: 450 us -> 78.3 us
  waiting for transfers between devices: 168 us -> 20.5 us
  matrix products: 109 us -> 6.9 us
  local copies, waits for them, and re-layouts: 98.2 us -> 0.05 us
  other arithmetic: 57.7 us -> 0.08 us
  Pallas kernels: 0 us -> 27.3 us
  starting transfers between devices: 3.5 us -> 23.2 us
  between operations: 14 us -> 0.15 us
    psum x1 -> x0, waiting for transfers between devices: 137 us -> none  [on_device(): lax.psum(collected.astype(jnp.float32).astype(jnp.bfloat16), 'chan')]
    conv_general_dilated x1 -> x0, matrix products: 56.7 us -> none  [whiten(): lax.conv_general_dilated(signal, kernel, (4,), [(fir_taps.shape[0] - 1, 0...]
    cos x2 -> x0, other arithmetic: 46.6 us -> none  [the longest x1 36.9 us: forward_table(): return jnp.concatenate([jnp.cos(angles), -jnp.sin(angles)], axis=1)]
    dot_general x7 -> x1, matrix products: 52.1 us -> 6.9 us  [dot(): return jnp.dot(a, b, preferred_element_type=jnp.float32)]
    reshape x3 -> x0, local copies, waits for them, and re-layouts: 44.4 us -> none  [the longest x2 44.3 us: whiten(): signal = records.reshape(channels * windows, 1, samples)]
    all_gather x1 -> x0, waiting for transfers between devices: 31.3 us -> none  [on_device(): lax.all_gather(selection.astype(jnp.bfloat16), 'tm', axis=1, tiled=True)]
    pallas_call x0 -> x7, Pallas kernels: none -> 27.3 us  [the longest x1 8.12 us: whitened_spectra(): pl.pallas_call(functools.partial(fir_kernel, windows=windows), in_specs=[...]
    ppermute x0 -> x19, starting transfers between devices: none -> 23.2 us  [shifted(): return lax.ppermute(value, axis, pairs)]
  transfers between devices with their start and end apart: 3 -> 19, of which waited for: 2 -> 11; matrix products, arithmetic and copies ran while one was open for 4% -> 0% of each run, Pallas kernels for 0% -> 9%
where the time goes in v1:
time: 78.4 us; the launch traced here: 78.3 us
  Pallas kernels  27.3 us (35%)
  starting transfers between devices  23.2 us (30%)
  waiting for transfers between devices  20.5 us (26%)
  matrix products  6.9 us (9%)
    ppermute x19, starting transfers between devices, shifted(): return lax.ppermute(value, axis, pairs)  23.2 us
    ppermute x19, waiting for transfers between devices, shifted(): return lax.ppermute(value, axis, pairs)  20.5 us
    pallas_call x1, Pallas kernels, whitened_spectra(): pl.pallas_call(functools.partial(fir_kernel, windows=windows), in_specs=[...  8.12 us
    pallas_call x2, Pallas kernels, crossed(): pl.pallas_call(functools.partial(cross_kernel, fetch=fetch, own=own, size...  7.43 us
    dot_general x1, matrix products, dot(): return jnp.dot(a, b, preferred_element_type=jnp.float32)  6.9 us
    pallas_call x1, Pallas kernels, correlations(): pl.pallas_call(functools.partial(lag_kernel, scale=1.0 / math.sqrt(NFREQ...  6.42 us
    pallas_call x1, Pallas kernels, expanded_local(): pl.pallas_call(functools.partial(expand_kernel, sizes=sizes), out_shape=j...  3.71 us
  transfers between devices with their start and end apart: 19, of which 11 were waited for; matrix products, arithmetic and copies ran while one was open for 0% of the time, Pallas kernels for 9%

profile of v1, /device:TPU:0, one launch (start us, length us, event | category | flops | bytes accessed | tf_op | source)
XLA Modules:
  0.0 78.3 jit_solution(14772554116184292378)
XLA Ops:
  0.0 8.1 %fir.1 = bf16[8,192,1536]{2,1,0:T(8,128)(2,1)} custom-call(bf16[192,16384]{1,0:T(8,128)(2,1)} %bitcast.13, bf16[1,32]{1,0:T(2,128)(2,1)} %bitcast.14), custom_call_target="tpu_custom_call" | custom-call | tf_op jit(solution)/shard_map/fir/pallas_call | solution.py:226
  8.1 6.9 %fusion.part_ref = f32[8,192,1024]{2,1,0:T(8,128)S(1)} fusion(bf16[8,192,1536]{2,1,0:T(8,128)(2,1)} %fir.1, bf16[1536,1024,1]{1,0,2:T(8,128)(2,1)S(1)} %copy-done.2), kind=kOutput, calls=%fused_computation.1 | convolution fusion | flops 4831838208 | bytes 14155776 | tf_op jit(solution)/shard_map/dot_general | solution.py:48
  15.1 1.4 %whiten.1 = (bf16[2,192,128]{2,1,0:T(8,128)(2,1)S(1)}, bf16[2,192,128]{2,1,0:T(8,128)(2,1)S(1)}, bf16[2,192,128]{2,1,0:T(8,128)(2,1)S(1)}, bf16[2,192,128]{2,1,0...) custom-call(f32[8,192,1024]{2,1,0:T(8,128)S(1)} %fusion.part_ref), custom_call_target="tpu_custom_call" | custom-call | tf_op jit(solution)/shard_map/whiten/pallas_call | solution.py:240
  16.4 3.1 %collective-permute-start = (bf16[2,192,128]{2,1,0:T(8,128)(2,1)S(1)}, bf16[2,192,128]{2,1,0:T(8,128)(2,1)S(1)}, u32[]{:S(2)}, u32[]{:S(2)}) collective-permute-start(bf16[2,192,128]{2,1,0:T(8,128)(2,1)S(1)} %get-tuple-element.30), channel_id=1, source_target_pairs={{0,2},{1,3},{2,4},{3,5},{4,6},{5,7},{6,0},{7,1},{8,10},{9,11},{10,... | collective-permute-start | bytes 294920 | tf_op jit(solution)/shard_map/ppermute | solution.py:104
  19.5 2.6 %collective-permute-start.1 = (bf16[2,192,128]{2,1,0:T(8,128)(2,1)S(1)}, bf16[2,192,128]{2,1,0:T(8,128)(2,1)S(1)}, u32[]{:S(2)}, u32[]{:S(2)}) collective-permute-start(bf16[2,192,128]{2,1,0:T(8,128)(2,1)S(1)} %get-tuple-element.31), channel_id=1, source_target_pairs={{0,4},{1,5},{2,6},{3,7},{4,0},{5,1},{6,2},{7,3},{8,12},{9,13},{10,... | collective-permute-start | bytes 294920 | tf_op jit(solution)/shard_map/ppermute | solution.py:104
  22.1 1.3 %collective-permute-start.2 = (bf16[2,192,128]{2,1,0:T(8,128)(2,1)S(1)}, bf16[2,192,128]{2,1,0:T(8,128)(2,1)S(1)}, u32[]{:S(2)}, u32[]{:S(2)}) collective-permute-start(bf16[2,192,128]{2,1,0:T(8,128)(2,1)S(1)} %get-tuple-element.32), channel_id=1, source_target_pairs={{0,6},{1,7},{2,0},{3,1},{4,2},{5,3},{6,4},{7,5},{8,14},{9,15},{10,... | collective-permute-start | bytes 294920 | tf_op jit(solution)/shard_map/ppermute | solution.py:104
  23.5 1.5 %collective-permute-start.4 = (bf16[3,16,1024]{2,1,0:T(8,128)(2,1)S(1)}, bf16[3,16,1024]{2,1,0:T(8,128)(2,1)S(1)}, u32[]{:S(2)}, u32[]{:S(2)}) collective-permute-start(bf16[3,16,1024]{2,1,0:T(8,128)(2,1)S(1)} %get-tuple-element.35), channel_id=1, source_target_pairs={{0,16},{8,24},{16,0},{24,8},{1,17},{9,25},{17,1},{25,9},{2,18},{10... | collective-permute-start | bytes 294920 | tf_op jit(solution)/shard_map/ppermute | solution.py:104
  25.3 3.4 %collective-permute-done.1.refs_2_ = bf16[2,192,128]{2,1,0:T(8,128)(2,1)S(1)} collective-permute-done((bf16[2,192,128]{2,1,0:T(8,128)(2,1)S(1)}, bf16[2,192,128]{2,1,0:T(8,128)(2,1)S(1)}, u32[]{:S(2)}, u32[]{:S(2)}) %collective-permute-start.1) | collective-permute-done | bytes 98336 | tf_op jit(solution)/shard_map/ppermute | solution.py:104
  29.0 1.3 %collective-permute-done.5.refs_3_ = bf16[3,16,1024]{2,1,0:T(8,128)(2,1)S(1)} collective-permute-done((bf16[3,16,1024]{2,1,0:T(8,128)(2,1)S(1)}, bf16[3,16,1024]{2,1,0:T(8,128)(2,1)S(1)}, u32[]{:S(2)}, u32[]{:S(2)}) %collective-permute-start.5) | collective-permute-done | bytes 98336 | tf_op jit(solution)/shard_map/ppermute | solution.py:104
  30.7 1.6 %collective-permute-start.6 = (bf16[1,3,128,128]{3,2,1,0:T(8,128)(2,1)S(1)}, bf16[1,3,128,128]{3,2,1,0:T(8,128)(2,1)S(1)}, u32[]{:S(2)}, u32[]{:S(2)}) collective-permute-start(bf16[1,3,128,128]{3,2,1,0:T(8,128)(2,1)S(1)} %get-tuple-element.42), channel_id=1, source_target_pairs={{0,1},{1,0},{2,3},{3,2},{4,5},{5,4},{6,7},{7,6},{8,9},{9,8},{10,11... | collective-permute-start | bytes 294920 | tf_op jit(solution)/shard_map/ppermute | solution.py:104
  32.3 3.4 %collective-permute-done.6 = bf16[1,3,128,128]{3,2,1,0:T(8,128)(2,1)S(1)} collective-permute-done((bf16[1,3,128,128]{3,2,1,0:T(8,128)(2,1)S(1)}, bf16[1,3,128,128]{3,2,1,0:T(8,128)(2,1)S(1)}, u32[]{:S(2)}, u32[]{:S(2)}) %collective-permute-start.6) | collective-permute-done | bytes 98336 | tf_op jit(solution)/shard_map/ppermute | solution.py:104
  35.7 1.7 %collective-permute-start.9 = (bf16[1,3,128,128]{3,2,1,0:T(8,128)(2,1)S(1)}, bf16[1,3,128,128]{3,2,1,0:T(8,128)(2,1)S(1)}, u32[]{:S(2)}, u32[]{:S(2)}) collective-permute-start(bf16[1,3,128,128]{3,2,1,0:T(8,128)(2,1)S(1)} %add.3), channel_id=1, source_target_pairs={{0,6},{1,7},{2,0},{3,1},{4,2},{5,3},{6,4},{7,5},{8,14},{9,15},{10,... | collective-permute-start | bytes 294920 | tf_op jit(solution)/shard_map/ppermute | solution.py:104
  37.4 3.3 %collective-permute-start.8 = (bf16[1,3,128,128]{3,2,1,0:T(8,128)(2,1)S(1)}, bf16[1,3,128,128]{3,2,1,0:T(8,128)(2,1)S(1)}, u32[]{:S(2)}, u32[]{:S(2)}) collective-permute-start(bf16[1,3,128,128]{3,2,1,0:T(8,128)(2,1)S(1)} %add.3), channel_id=1, source_target_pairs={{0,4},{1,5},{2,6},{3,7},{4,0},{5,1},{6,2},{7,3},{8,12},{9,13},{10,... | collective-permute-start | bytes 294920 | tf_op jit(solution)/shard_map/ppermute | solution.py:104
  40.8 1.9 %collective-permute-start.7 = (bf16[1,3,128,128]{3,2,1,0:T(8,128)(2,1)S(1)}, bf16[1,3,128,128]{3,2,1,0:T(8,128)(2,1)S(1)}, u32[]{:S(2)}, u32[]{:S(2)}) collective-permute-start(bf16[1,3,128,128]{3,2,1,0:T(8,128)(2,1)S(1)} %add.3), channel_id=1, source_target_pairs={{0,2},{1,3},{2,4},{3,5},{4,6},{5,7},{6,0},{7,1},{8,10},{9,11},{10,... | collective-permute-start | bytes 294920 | tf_op jit(solution)/shard_map/ppermute | solution.py:104
  42.7 6.5 %collective-permute-done.8 = bf16[1,3,128,128]{3,2,1,0:T(8,128)(2,1)S(1)} collective-permute-done((bf16[1,3,128,128]{3,2,1,0:T(8,128)(2,1)S(1)}, bf16[1,3,128,128]{3,2,1,0:T(8,128)(2,1)S(1)}, u32[]{:S(2)}, u32[]{:S(2)}) %collective-permute-start.8) | collective-permute-done | bytes 98336 | tf_op jit(solution)/shard_map/ppermute | solution.py:104
  49.4 1.6 %collective-permute-start.10 = (bf16[4,3,128,128]{3,2,1,0:T(8,128)(2,1)S(1)}, bf16[4,3,128,128]{3,2,1,0:T(8,128)(2,1)S(1)}, u32[]{:S(2)}, u32[]{:S(2)}) collective-permute-start(bf16[4,3,128,128]{3,2,1,0:T(8,128)(2,1)S(1)} %pad_maximum_fusion.refs_0_), channel_id=1, source_target_pairs={{0,1},{1,0},{2,3},{3,2},{4,5},{5,4},{6,7},{7,6},{8,9},{9,8},{10,11... | collective-permute-start | bytes 1179656 | tf_op jit(solution)/shard_map/ppermute | solution.py:104
  51.0 3.7 %expand.1 = bf16[64,16,16,192]{3,2,1,0:T(8,128)(2,1)S(1)} custom-call(bf16[3,16,1024]{2,1,0:T(8,128)(2,1)S(1)} %get-tuple-element.43.refs_0_, bf16[3,16,1024]{2,1,0:T(8,128)(2,1)S(1)} %collective-permute-done.3.refs_1_, bf16[3,16,1024]{2,1,0:T(8,128)(2,1)S(1)} %collective-permute-done.4.refs_2_, bf16[3,16,1024]{2,1,0:T(8,128)(2,1)S(1)} %collective-permute-done.5.refs_3_), custom_call_target="tpu_custom_call" | custom-call | flops 4000000000 | bytes 8388608 | tf_op jit(solution)/shard_map/expand/pallas_call | solution.py:331
  54.8 2.8 %collective-permute-done.11.refs_2_ = bf16[4,3,128,128]{3,2,1,0:T(8,128)(2,1)S(1)} collective-permute-done((bf16[4,3,128,128]{3,2,1,0:T(8,128)(2,1)S(1)}, bf16[4,3,128,128]{3,2,1,0:T(8,128)(2,1)S(1)}, u32[]{:S(2)}, u32[]{:S(2)}) %collective-permute-start.11) | collective-permute-done | bytes 393248 | tf_op jit(solution)/shard_map/ppermute | solution.py:104
  58.2 1.5 %collective-permute-start.14 = (bf16[4,3,64,128]{3,2,1,0:T(8,128)(2,1)S(1)}, bf16[4,3,64,128]{3,2,1,0:T(8,128)(2,1)S(1)}, u32[]{:S(2)}, u32[]{:S(2)}) collective-permute-start(bf16[4,3,64,128]{3,2,1,0:T(8,128)(2,1)S(1)} %slice.7), channel_id=1, source_target_pairs={{0,1},{1,0},{2,3},{3,2},{4,5},{5,4},{6,7},{7,6},{8,9},{9,8},{10,11... | collective-permute-start | bytes 589832 | tf_op jit(solution)/shard_map/ppermute | solution.py:104
  59.8 1.7 %collective-permute-start.13 = (bf16[4,3,64,128]{3,2,1,0:T(8,128)(2,1)S(1)}, bf16[4,3,64,128]{3,2,1,0:T(8,128)(2,1)S(1)}, u32[]{:S(2)}, u32[]{:S(2)}) collective-permute-start(bf16[4,3,64,128]{3,2,1,0:T(8,128)(2,1)S(1)} %slice.6), channel_id=1, source_target_pairs={{0,16},{8,24},{16,0},{24,8},{1,17},{9,25},{17,1},{25,9},{2,18},{10... | collective-permute-start | bytes 589832 | tf_op jit(solution)/shard_map/ppermute | solution.py:104
  61.4 3.7 %cross.2.refs_6_ = bf16[2048,1024]{1,0:T(8,128)(2,1)S(1)} custom-call(bf16[64,256,192]{2,1,0:T(8,128)(2,1)S(1)} %bitcast.10, bf16[4,3,128,128]{3,2,1,0:T(8,128)(2,1)S(1)} %pad_maximum_fusion.refs_0_, bf16[4,3,128,128]{3,2,1,0:T(8,128)(2,1)S(1)} %collective-permute-done.15.refs_1_, bf16[4,3,128,128]{3,2,1,0:T(8,128)(2,1)S(1)} %collective-permute-done.11.refs_2_, ...), custom_call_target="tpu_custom_call" | custom-call | flops 4000000000 | bytes 8388608 | tf_op jit(solution)/shard_map/cross/pallas_call | solution.py:378
  65.1 1.2 %collective-permute-done.13.refs_2_ = bf16[4,3,64,128]{3,2,1,0:T(8,128)(2,1)S(1)} collective-permute-done((bf16[4,3,64,128]{3,2,1,0:T(8,128)(2,1)S(1)}, bf16[4,3,64,128]{3,2,1,0:T(8,128)(2,1)S(1)}, u32[]{:S(2)}, u32[]{:S(2)}) %collective-permute-start.13) | collective-permute-done | bytes 196640 | tf_op jit(solution)/shard_map/ppermute | solution.py:104
  68.1 3.7 %cross.3.cross_ref = bf16[2048,1024]{1,0:T(8,128)(2,1)S(1)} custom-call(bf16[64,256,192]{2,1,0:T(8,128)(2,1)S(1)} %bitcast.11, bf16[4,3,128,128]{3,2,1,0:T(8,128)(2,1)S(1)} %collective-permute-done.10.refs_0_, bf16[4,3,128,128]{3,2,1,0:T(8,128)(2,1)S(1)} %collective-permute-done.12.refs_1_, ...), custom_call_target="tpu_custom_call", output_to_operand_aliasing={{}: (7, {})} | custom-call | flops 4000000000 | bytes 8388608 | tf_op jit(solution)/shard_map/cross/pallas_call | solution.py:378
  71.8 6.4 %lags.1 = f32[2048,1024]{1,0:T(8,128)} custom-call(bf16[2048,1024]{1,0:T(8,128)(2,1)S(1)} %cross.3.cross_ref, bf16[1024,1024]{1,0:T(8,128)(2,1)S(1)} %copy-done), custom_call_target="tpu_custom_call" | custom-call | tf_op jit(solution)/shard_map/lags/pallas_call | solution.py:422
  (32 shorter events, 3.7 us)
Async XLA Ops:
  0.0 8.1 %copy-start.2 = (bf16[1536,1024,1]{1,0,2:T(8,128)(2,1)S(1)}, bf16[1536,1024,1]{1,0,2:T(8,128)(2,1)}, u32[]{:S(2)}) copy-start(bf16[1536,1024,1]{1,0,2:T(8,128)(2,1)} %constant.7) | copy-start | bytes 9437188
  15.1 15.3 %copy-start.1 = (s32[128]{0:T(128)S(1)}, s32[128]{0:T(128)}, u32[]{:S(2)}) copy-start(s32[128]{0:T(128)} %param.7) | copy-start | bytes 1540
  16.4 8.8 %collective-permute-start = (bf16[2,192,128]{2,1,0:T(8,128)(2,1)S(1)}, bf16[2,192,128]{2,1,0:T(8,128)(2,1)S(1)}, u32[]{:S(2)}, u32[]{:S(2)}) collective-permute-start(bf16[2,192,128]{2,1,0:T(8,128)(2,1)S(1)} %get-tuple-element.30), channel_id=1, source_target_pairs={{0,2},{1,3},{2,4},{3,5},{4,6},{5,7},{6,0},{7,1},{8,10},{9,11},{10,... | collective-permute-start | bytes 294920 | tf_op jit(solution)/shard_map/ppermute | solution.py:104
  19.5 9.2 %collective-permute-start.1 = (bf16[2,192,128]{2,1,0:T(8,128)(2,1)S(1)}, bf16[2,192,128]{2,1,0:T(8,128)(2,1)S(1)}, u32[]{:S(2)}, u32[]{:S(2)}) collective-permute-start(bf16[2,192,128]{2,1,0:T(8,128)(2,1)S(1)} %get-tuple-element.31), channel_id=1, source_target_pairs={{0,4},{1,5},{2,6},{3,7},{4,0},{5,1},{6,2},{7,3},{8,12},{9,13},{10,... | collective-permute-start | bytes 294920 | tf_op jit(solution)/shard_map/ppermute | solution.py:104
  22.1 6.6 %collective-permute-start.2 = (bf16[2,192,128]{2,1,0:T(8,128)(2,1)S(1)}, bf16[2,192,128]{2,1,0:T(8,128)(2,1)S(1)}, u32[]{:S(2)}, u32[]{:S(2)}) collective-permute-start(bf16[2,192,128]{2,1,0:T(8,128)(2,1)S(1)} %get-tuple-element.32), channel_id=1, source_target_pairs={{0,6},{1,7},{2,0},{3,1},{4,2},{5,3},{6,4},{7,5},{8,14},{9,15},{10,... | collective-permute-start | bytes 294920 | tf_op jit(solution)/shard_map/ppermute | solution.py:104
  23.4 5.3 %collective-permute-start.3 = (bf16[3,16,1024]{2,1,0:T(8,128)(2,1)S(1)}, bf16[3,16,1024]{2,1,0:T(8,128)(2,1)S(1)}, u32[]{:S(2)}, u32[]{:S(2)}) collective-permute-start(bf16[3,16,1024]{2,1,0:T(8,128)(2,1)S(1)} %get-tuple-element.34), channel_id=1, source_target_pairs={{0,8},{8,0},{16,24},{24,16},{1,9},{9,1},{17,25},{25,17},{2,10},{10... | collective-permute-start | bytes 294920 | tf_op jit(solution)/shard_map/ppermute | solution.py:104
  23.5 5.6 %collective-permute-start.4 = (bf16[3,16,1024]{2,1,0:T(8,128)(2,1)S(1)}, bf16[3,16,1024]{2,1,0:T(8,128)(2,1)S(1)}, u32[]{:S(2)}, u32[]{:S(2)}) collective-permute-start(bf16[3,16,1024]{2,1,0:T(8,128)(2,1)S(1)} %get-tuple-element.35), channel_id=1, source_target_pairs={{0,16},{8,24},{16,0},{24,8},{1,17},{9,25},{17,1},{25,9},{2,18},{10... | collective-permute-start | bytes 294920 | tf_op jit(solution)/shard_map/ppermute | solution.py:104
  25.2 5.2 %collective-permute-start.5 = (bf16[3,16,1024]{2,1,0:T(8,128)(2,1)S(1)}, bf16[3,16,1024]{2,1,0:T(8,128)(2,1)S(1)}, u32[]{:S(2)}, u32[]{:S(2)}) collective-permute-start(bf16[3,16,1024]{2,1,0:T(8,128)(2,1)S(1)} %get-tuple-element.36), channel_id=1, source_target_pairs={{0,24},{8,16},{16,8},{24,0},{1,25},{9,17},{17,9},{25,1},{2,26},{10... | collective-permute-start | bytes 294920 | tf_op jit(solution)/shard_map/ppermute | solution.py:104
  30.7 5.0 %collective-permute-start.6 = (bf16[1,3,128,128]{3,2,1,0:T(8,128)(2,1)S(1)}, bf16[1,3,128,128]{3,2,1,0:T(8,128)(2,1)S(1)}, u32[]{:S(2)}, u32[]{:S(2)}) collective-permute-start(bf16[1,3,128,128]{3,2,1,0:T(8,128)(2,1)S(1)} %get-tuple-element.42), channel_id=1, source_target_pairs={{0,1},{1,0},{2,3},{3,2},{4,5},{5,4},{6,7},{7,6},{8,9},{9,8},{10,11... | collective-permute-start | bytes 294920 | tf_op jit(solution)/shard_map/ppermute | solution.py:104
  35.7 7.0 %collective-permute-start.9 = (bf16[1,3,128,128]{3,2,1,0:T(8,128)(2,1)S(1)}, bf16[1,3,128,128]{3,2,1,0:T(8,128)(2,1)S(1)}, u32[]{:S(2)}, u32[]{:S(2)}) collective-permute-start(bf16[1,3,128,128]{3,2,1,0:T(8,128)(2,1)S(1)} %add.3), channel_id=1, source_target_pairs={{0,6},{1,7},{2,0},{3,1},{4,2},{5,3},{6,4},{7,5},{8,14},{9,15},{10,... | collective-permute-start | bytes 294920 | tf_op jit(solution)/shard_map/ppermute | solution.py:104
  37.4 11.8 %collective-permute-start.8 = (bf16[1,3,128,128]{3,2,1,0:T(8,128)(2,1)S(1)}, bf16[1,3,128,128]{3,2,1,0:T(8,128)(2,1)S(1)}, u32[]{:S(2)}, u32[]{:S(2)}) collective-permute-start(bf16[1,3,128,128]{3,2,1,0:T(8,128)(2,1)S(1)} %add.3), channel_id=1, source_target_pairs={{0,4},{1,5},{2,6},{3,7},{4,0},{5,1},{6,2},{7,3},{8,12},{9,13},{10,... | collective-permute-start | bytes 294920 | tf_op jit(solution)/shard_map/ppermute | solution.py:104
  40.8 8.5 %collective-permute-start.7 = (bf16[1,3,128,128]{3,2,1,0:T(8,128)(2,1)S(1)}, bf16[1,3,128,128]{3,2,1,0:T(8,128)(2,1)S(1)}, u32[]{:S(2)}, u32[]{:S(2)}) collective-permute-start(bf16[1,3,128,128]{3,2,1,0:T(8,128)(2,1)S(1)} %add.3), channel_id=1, source_target_pairs={{0,2},{1,3},{2,4},{3,5},{4,6},{5,7},{6,0},{7,1},{8,10},{9,11},{10,... | collective-permute-start | bytes 294920 | tf_op jit(solution)/shard_map/ppermute | solution.py:104
  49.3 8.2 %collective-permute-start.11 = (bf16[4,3,128,128]{3,2,1,0:T(8,128)(2,1)S(1)}, bf16[4,3,128,128]{3,2,1,0:T(8,128)(2,1)S(1)}, u32[]{:S(2)}, u32[]{:S(2)}) collective-permute-start(bf16[4,3,128,128]{3,2,1,0:T(8,128)(2,1)S(1)} %pad_maximum_fusion.refs_0_), channel_id=1, source_target_pairs={{0,16},{8,24},{16,0},{24,8},{1,17},{9,25},{17,1},{25,9},{2,18},{10... | collective-permute-start | bytes 1179656 | tf_op jit(solution)/shard_map/ppermute | solution.py:104
  49.4 8.2 %collective-permute-start.10 = (bf16[4,3,128,128]{3,2,1,0:T(8,128)(2,1)S(1)}, bf16[4,3,128,128]{3,2,1,0:T(8,128)(2,1)S(1)}, u32[]{:S(2)}, u32[]{:S(2)}) collective-permute-start(bf16[4,3,128,128]{3,2,1,0:T(8,128)(2,1)S(1)} %pad_maximum_fusion.refs_0_), channel_id=1, source_target_pairs={{0,1},{1,0},{2,3},{3,2},{4,5},{5,4},{6,7},{7,6},{8,9},{9,8},{10,11... | collective-permute-start | bytes 1179656 | tf_op jit(solution)/shard_map/ppermute | solution.py:104
  54.7 6.7 %collective-permute-start.15 = (bf16[4,3,128,128]{3,2,1,0:T(8,128)(2,1)S(1)}, bf16[4,3,128,128]{3,2,1,0:T(8,128)(2,1)S(1)}, u32[]{:S(2)}, u32[]{:S(2)}) collective-permute-start(bf16[4,3,128,128]{3,2,1,0:T(8,128)(2,1)S(1)} %pad_maximum_fusion.refs_0_), channel_id=1, source_target_pairs={{0,8},{8,0},{16,24},{24,16},{1,9},{9,1},{17,25},{25,17},{2,10},{10... | collective-permute-start | bytes 1179656 | tf_op jit(solution)/shard_map/ppermute | solution.py:104
  57.6 3.8 %collective-permute-start.16 = (bf16[4,3,128,128]{3,2,1,0:T(8,128)(2,1)S(1)}, bf16[4,3,128,128]{3,2,1,0:T(8,128)(2,1)S(1)}, u32[]{:S(2)}, u32[]{:S(2)}) collective-permute-start(bf16[4,3,128,128]{3,2,1,0:T(8,128)(2,1)S(1)} %collective-permute-done.11.refs_2_), channel_id=1, source_target_pairs={{0,8},{8,0},{16,24},{24,16},{1,9},{9,1},{17,25},{25,17},{2,10},{10... | collective-permute-start | bytes 1179656 | tf_op jit(solution)/shard_map/ppermute | solution.py:104
  57.7 9.2 %collective-permute-start.12 = (bf16[4,3,128,128]{3,2,1,0:T(8,128)(2,1)S(1)}, bf16[4,3,128,128]{3,2,1,0:T(8,128)(2,1)S(1)}, u32[]{:S(2)}, u32[]{:S(2)}) collective-permute-start(bf16[4,3,128,128]{3,2,1,0:T(8,128)(2,1)S(1)} %collective-permute-done.10.refs_0_), channel_id=1, source_target_pairs={{0,8},{8,0},{16,24},{24,16},{1,9},{9,1},{17,25},{25,17},{2,10},{10... | collective-permute-start | bytes 1179656 | tf_op jit(solution)/shard_map/ppermute | solution.py:104
  58.2 6.9 %collective-permute-start.14 = (bf16[4,3,64,128]{3,2,1,0:T(8,128)(2,1)S(1)}, bf16[4,3,64,128]{3,2,1,0:T(8,128)(2,1)S(1)}, u32[]{:S(2)}, u32[]{:S(2)}) collective-permute-start(bf16[4,3,64,128]{3,2,1,0:T(8,128)(2,1)S(1)} %slice.7), channel_id=1, source_target_pairs={{0,1},{1,0},{2,3},{3,2},{4,5},{5,4},{6,7},{7,6},{8,9},{9,8},{10,11... | collective-permute-start | bytes 589832 | tf_op jit(solution)/shard_map/ppermute | solution.py:104
  59.8 6.6 %collective-permute-start.13 = (bf16[4,3,64,128]{3,2,1,0:T(8,128)(2,1)S(1)}, bf16[4,3,64,128]{3,2,1,0:T(8,128)(2,1)S(1)}, u32[]{:S(2)}, u32[]{:S(2)}) collective-permute-start(bf16[4,3,64,128]{3,2,1,0:T(8,128)(2,1)S(1)} %slice.6), channel_id=1, source_target_pairs={{0,16},{8,24},{16,0},{24,8},{1,17},{9,25},{17,1},{25,9},{2,18},{10... | collective-permute-start | bytes 589832 | tf_op jit(solution)/shard_map/ppermute | solution.py:104
  65.1 6.7 %copy-start = (bf16[1024,1024]{1,0:T(8,128)(2,1)S(1)}, bf16[1024,1024]{1,0:T(8,128)(2,1)}, u32[]{:S(2)}) copy-start(bf16[1024,1024]{1,0:T(8,128)(2,1)} %constant.5.clone.table_ref) | copy-start | bytes 6291460
  66.4 1.4 %collective-permute-start.17 = (bf16[4,3,64,128]{3,2,1,0:T(8,128)(2,1)S(1)}, bf16[4,3,64,128]{3,2,1,0:T(8,128)(2,1)S(1)}, u32[]{:S(2)}, u32[]{:S(2)}) collective-permute-start(bf16[4,3,64,128]{3,2,1,0:T(8,128)(2,1)S(1)} %collective-permute-done.13.refs_2_), channel_id=1, source_target_pairs={{0,8},{8,0},{16,24},{24,16},{1,9},{9,1},{17,25},{25,17},{2,10},{10... | collective-permute-start | bytes 589832 | tf_op jit(solution)/shard_map/ppermute | solution.py:104
  66.4 1.7 %collective-permute-start.18 = (bf16[4,3,64,128]{3,2,1,0:T(8,128)(2,1)S(1)}, bf16[4,3,64,128]{3,2,1,0:T(8,128)(2,1)S(1)}, u32[]{:S(2)}, u32[]{:S(2)}) collective-permute-start(bf16[4,3,64,128]{3,2,1,0:T(8,128)(2,1)S(1)} %collective-permute-done.14.refs_3_), channel_id=1, source_target_pairs={{0,8},{8,0},{16,24},{24,16},{1,9},{9,1},{17,25},{25,17},{2,10},{10... | collective-permute-start | bytes 589832 | tf_op jit(solution)/shard_map/ppermute | solution.py:104

commit v2 on v1

--- a/solution.py
+++ b/solution.py
@@ -104,6 +104,21 @@
     return lax.ppermute(value, axis, pairs)
 
 
+def filter_matrix(taps, toeplitz):
+    in_index = lax.broadcasted_iota(jnp.int32, (256, 128), 0)
+    out_index = lax.broadcasted_iota(jnp.int32, (256, 128), 1)
+    tap = in_index - 4 * (out_index % TAPS) - 97
+    small = jnp.zeros((256, 128), jnp.float32)
+    for j in range(TAPS):
+        small = jnp.where(tap == j, taps[0:1, j : j + 1], small)
+    slot = lax.broadcasted_iota(jnp.int32, (128, 128), 1) // TAPS
+    for a in range(FIR_IN // 128):
+        for n in range(FIR_OUT // 128):
+            here = jnp.where(slot + n * (128 // TAPS) == a, small[:128], 0.0)
+            here = jnp.where(slot + n * (128 // TAPS) == a - 1, small[128:], here)
+            toeplitz[a * 128 : (a + 1) * 128, n * 128 : (n + 1) * 128] = here.astype(jnp.bfloat16)
+
+
 def fir_kernel(x_hbm, fir_hbm, out_ref, x_ref, fir_ref, toeplitz, sems, *, windows):
     chans = x_ref.shape[0] // windows
     fetch_fir = pltpu.make_async_copy(fir_hbm, fir_ref, sems.at[windows])
@@ -113,21 +128,8 @@
         mine = pl.ds(w * chans, chans)
         fetches.append(pltpu.make_async_copy(x_hbm.at[mine], x_ref.at[mine], sems.at[w]))
         fetches[-1].start()
-    in_index = lax.broadcasted_iota(jnp.int32, (256, 128), 0)
-    out_index = lax.broadcasted_iota(jnp.int32, (256, 128), 1)
-    tap = in_index - 4 * (out_index % TAPS) - 97
-    small = jnp.zeros((256, 128), jnp.float32)
     fetch_fir.wait()
-    taps = fir_ref[...].astype(jnp.float32)
-    for j in range(TAPS):
-        small = jnp.where(tap == j, taps[0:1, j : j + 1], small)
-    slot = lax.broadcasted_iota(jnp.int32, (128, 128), 1) // TAPS
-    for a in range(FIR_IN // 128):
-        for n in range(FIR_OUT // 128):
-            here = jnp.where(slot + n * (128 // TAPS) == a, small[:128], 0.0)
-            here = jnp.where(slot + n * (128 // TAPS) == a - 1, small[128:], here)
-            toeplitz[a * 128 : (a + 1) * 128, n * 128 : (n + 1) * 128] = here.astype(jnp.bfloat16)
-
+    filter_matrix(fir_ref[...].astype(jnp.float32), toeplitz)
     step = 4 * FIR_OUT
     per = SUB // FIR_OUT
     together = 4
@@ -223,12 +225,15 @@
     own = chans // tm_count
     x = jnp.transpose(strain, (1, 0, 2)).reshape(rows, samples)
     blocks = WIN // SUB
-    filtered = pl.pallas_call(
+    filtered, _ = pl.pallas_call(
         functools.partial(fir_kernel, windows=windows),
         in_specs=[pl.BlockSpec(memory_space=pl.ANY)] * 2,
-        out_shape=jax.ShapeDtypeStruct((blocks, rows, 3 * SUB), jnp.bfloat16),
+        out_specs=[pl.BlockSpec(memory_space=pltpu.VMEM)] * 2,
+        out_shape=[
+            jax.ShapeDtypeStruct((blocks, rows, 3 * SUB), jnp.bfloat16),
+            jax.ShapeDtypeStruct((rows, samples), jnp.bfloat16),
+        ],
         scratch_shapes=[
-            pltpu.VMEM((rows, samples), jnp.bfloat16),
             pltpu.VMEM((1, TAPS), jnp.bfloat16),
             pltpu.VMEM((FIR_IN, FIR_OUT), jnp.bfloat16),
             pltpu.SemaphoreType.DMA((windows + 1,)),
@@ -338,9 +343,9 @@
     return out.reshape(SPEC // (2 * GROUP), own * 2 * GROUP, depth)
 
 
-def cross_kernel(local_ref, *refs, fetch, own, sizes, by_y, aliased):
-    sources = refs[: len(refs) - 2 - aliased]
-    out_ref, wide = refs[-2:]
+def cross_kernel(local_ref, *refs, fetch, own, sizes, by_y):
+    sources = refs[:-1]
+    out_ref = refs[-1]
     count = sources[0].shape[-1]
     groups = 128 // (2 * GROUP)
     row = lax.broadcasted_iota(jnp.int32, (count, count), 0)
@@ -359,39 +364,60 @@
             [x[c * 2 * GROUP : (c + 1) * 2 * GROUP] for c in range(own) for x in cross], axis=0
         )
         turned = dot_nt(identity, tall)
-        for c in range(own):
-            wide[pl.ds(c, count, stride=own), :] = turned[:, c * 128 : (c + 1) * 128]
-        lanes = pl.ds(pl.multiple_of(block_at(sizes, step, -1) * 128, 128), 128)
-        out_ref[:, lanes] = wide[...].astype(jnp.bfloat16)
+        by_channel = jnp.stack([turned[:, c * 128 : (c + 1) * 128] for c in range(own)], axis=0)
+        mixed = jnp.transpose(by_channel, (1, 0, 2)).reshape(count * own, 128)
+        block = step if sizes is None else lax.div(block_at(sizes, step, -1), sizes["y"])
+        out_ref[:, pl.ds(pl.multiple_of(block * 128, 128), 128)] = mixed.astype(jnp.bfloat16)
         return carry
 
     lax.fori_loop(0, SPEC // 128 if by_y is None else sizes["z"], body, 0)
 
 
-def crossed(local, sources, fetch, sizes, by_y=None, held=None):
+def crossed(local, sources, fetch, sizes, by_y=None):
     _, expanded_rows, _ = local.shape
     own = expanded_rows // (2 * GROUP)
     count = sources[0].shape[-1]
-    shape = jax.ShapeDtypeStruct((count * own, SPEC), jnp.bfloat16)
-    extra = [] if held is None else [held]
-    specs = [pl.BlockSpec(memory_space=pltpu.VMEM)] * (1 + len(sources))
+    columns = SPEC if by_y is None else 128 * sizes["z"]
     return pl.pallas_call(
-        functools.partial(
-            cross_kernel, fetch=fetch, own=own, sizes=sizes, by_y=by_y, aliased=len(extra)
-        ),
-        in_specs=specs + [pl.BlockSpec(memory_space=pltpu.VMEM)] * len(extra),
-        out_shape=shape,
-        input_output_aliases={1 + len(sources): 0} if extra else {},
-        scratch_shapes=[pltpu.VMEM((count * own, 128), jnp.float32)],
+        functools.partial(cross_kernel, fetch=fetch, own=own, sizes=sizes, by_y=by_y),
+        out_shape=jax.ShapeDtypeStruct((count * own, columns), jnp.bfloat16),
         cost_estimate=pl.CostEstimate(flops=4 * 10**9, bytes_accessed=8 * MIB, transcendentals=0),
         compiler_params=pltpu.CompilerParams(vmem_limit_bytes=32 * MIB),
         name="cross",
-    )(local, *sources, *extra)
-
-
-def lag_kernel(cross_ref, table_ref, out_hbm, buffer, sems, *, scale):
+    )(local, *sources)
+
+
+def table_rows(table_ref, columns, sizes, by_y):
+    if by_y is None:
+        return table_ref[...]
+    y = lax.rem(chan_at(sizes, 0, -by_y), sizes["y"])
+    rows = [pl.ds(pl.multiple_of((z * sizes["y"] + y) * 128, 128), 128) for z in range(columns // 128)]
+    return jnp.concatenate([table_ref[r] for r in rows], axis=0)
+
+
+def part_kernel(cross_ref, table_ref, out_ref, chosen, *, sizes, by_y):
+    chosen[...] = table_rows(table_ref, cross_ref.shape[1], sizes, by_y)
+    height = 512
+
+    def body(i, carry):
+        mine = pl.ds(pl.multiple_of(i * height, height), height)
+        rows = cross_ref[mine]
+        for n in range(LAGS // 256):
+            at = slice(n * 256, (n + 1) * 256)
+            out_ref[mine, at] = dot(rows, chosen[:, at])
+        return carry
+
+    lax.fori_loop(0, cross_ref.shape[0] // height, body, 0)
+
+
+def lag_kernel(*refs, scale, sizes, by_y):
+    cross_ref, table_ref = refs[:2]
+    chosen, buffer, sems = refs[-3:]
+    out_hbm = refs[-4]
+    earlier = refs[2:-4]
     depth, height, lags = buffer.shape
     steps = cross_ref.shape[0] // height
+    chosen[...] = table_rows(table_ref, cross_ref.shape[1], sizes, by_y)
 
     def store(i):
         mine = pl.ds(pl.multiple_of(i * height, height), height)
@@ -403,11 +429,15 @@
         def _():
             store(i - depth).wait()
 
-        rows = cross_ref[pl.ds(pl.multiple_of(i * height, height), height)]
+        mine = pl.ds(pl.multiple_of(i * height, height), height)
+        rows = cross_ref[mine]
         slot = lax.rem(i, depth)
         for n in range(lags // 256):
             at = slice(n * 256, (n + 1) * 256)
-            buffer[slot, :, at] = dot(rows, table_ref[:, at]) * scale
+            total = dot(rows, chosen[:, at])
+            for held in earlier:
+                total = total + held[mine, at]
+            buffer[slot, :, at] = total * scale
         store(i).start()
         return carry
 
@@ -416,25 +446,39 @@
         store(i).wait()
 
 
-def correlations(cross, source_count, window_total):
-    rows = cross.shape[0]
-    height = 512
-    out = pl.pallas_call(
-        functools.partial(lag_kernel, scale=1.0 / math.sqrt(NFREQ * window_total)),
-        in_specs=[pl.BlockSpec(memory_space=pltpu.VMEM)] * 2,
+def lag_parts(cross, sizes, by_y):
+    rows, columns = cross.shape
+    return pl.pallas_call(
+        functools.partial(part_kernel, sizes=sizes, by_y=by_y),
+        out_shape=jax.ShapeDtypeStruct((rows, LAGS), jnp.float32),
+        scratch_shapes=[pltpu.VMEM((columns, LAGS), jnp.bfloat16)],
+        cost_estimate=pl.CostEstimate(flops=4 * 10**9, bytes_accessed=8 * MIB, transcendentals=0),
+        compiler_params=pltpu.CompilerParams(vmem_limit_bytes=24 * MIB),
+        name="lags_near",
+    )(cross, jnp.asarray(lag_constant()))
+
+
+def correlations(cross, earlier, window_total, sizes=None, by_y=None):
+    rows, columns = cross.shape
+    height = 256
+    return pl.pallas_call(
+        functools.partial(
+            lag_kernel, scale=1.0 / math.sqrt(NFREQ * window_total), sizes=sizes, by_y=by_y
+        ),
+        in_specs=[pl.BlockSpec(memory_space=pltpu.VMEM)] * (2 + len(earlier)),
         out_specs=pl.BlockSpec(memory_space=pl.ANY),
         out_shape=jax.ShapeDtypeStruct((rows, LAGS), jnp.float32),
         scratch_shapes=[
-            pltpu.VMEM((2, height, LAGS), jnp.float32),
-            pltpu.SemaphoreType.DMA((2,)),
+            pltpu.VMEM((columns, LAGS), jnp.bfloat16),
+            pltpu.VMEM((3, height, LAGS), jnp.float32),
+            pltpu.SemaphoreType.DMA((3,)),
         ],
         compiler_params=pltpu.CompilerParams(vmem_limit_bytes=24 * MIB),
         name="lags",
-    )(cross, jnp.asarray(lag_constant()))
-    return out.reshape(source_count, -1, LAGS)
-
-
-def gathered(picked, local, sizes):
+    )(cross, jnp.asarray(lag_constant()), *earlier)
+
+
+def gathered(picked, local, window_total, sizes):
     windows, width = picked.shape[1:3]
     half = width // 2
     whole = jnp.concatenate([shifted(sizes, picked, z=d) for d in range(sizes["z"])], axis=0)
@@ -474,18 +518,19 @@
 
         return arrays, fetch
 
-    cross = None
+    earlier = []
     for y in range(sizes["y"]):
         if y > 0:
             far = {key: array for key, array in held.items() if key[0] and key[1]}
             far, cross = lax.optimization_barrier((far, cross))
             held.update(far)
+            earlier.append(lag_parts(cross, sizes, y - 1))
         arrays, fetch = rows_of(y)
-        cross = crossed(expanded, arrays, fetch, sizes, by_y=y, held=cross)
-    return cross
-
-
-def gathered_plainly(picked, local, sizes):
+        cross = crossed(expanded, arrays, fetch, sizes, by_y=y)
+    return correlations(cross, earlier, window_total, sizes, sizes["y"] - 1)
+
+
+def gathered_plainly(picked, local, window_total, sizes):
     parts = [shifted(sizes, picked, x=x, c=c) for x in range(sizes["x"]) for c in range(sizes["c"])]
     mine = jnp.concatenate(parts, axis=1)[0]
     total, width, count = mine.shape
@@ -496,7 +541,8 @@
     def fetch(refs, step):
         return [refs[0][step, i] for i in range(total)]
 
-    return crossed(expanded_local(local, None), [held], fetch, None)
+    cross = crossed(expanded_local(local, None), [held], fetch, None)
+    return correlations(cross, [], window_total)
 
 
 def on_device(strain_rate, fir_taps, source_channels):
@@ -509,8 +555,8 @@
     bins, local = lax.optimization_barrier((bins, local))
     picked = picked_sources(source_channels, bins, windows, sizes)
     gather = gathered if picked.shape[2] == 128 else gathered_plainly
-    cross = gather(picked, local, sizes)
-    return correlations(cross, source_channels.shape[0], windows * lax.axis_size("tm"))
+    out = gather(picked, local, windows * lax.axis_size("tm"), sizes)
+    return out.reshape(source_channels.shape[0], -1, LAGS)
 
 
 def solution(mesh):

time: 78.4 us -> 79.7 us (1.017)
  Pallas kernels: 27.3 us -> 29.3 us
    pallas_call x0 -> x1, Pallas kernels: none -> 2.91 us  [lag_parts(): pl.pallas_call(functools.partial(part_kernel, sizes=sizes, by_y=by_y), ou...]
    pallas_call x1, Pallas kernels: 8.12 us -> 9.93 us  [whitened_spectra(): pl.pallas_call(functools.partial(fir_kernel, windows=windows), in_specs=[...]
    pallas_call x1, Pallas kernels: 6.42 us -> 4.8 us  [correlations(): pl.pallas_call(functools.partial(lag_kernel, scale=1.0 / math.sqrt(NFREQ...]
    pallas_call x2, Pallas kernels: 7.43 us -> 6.29 us  [crossed(): pl.pallas_call(functools.partial(cross_kernel, fetch=fetch, own=own, size...]
  transfers between devices with their start and end apart: 19 -> 19, of which waited for: 11 -> 10; matrix products, arithmetic and copies ran while one was open for 0% -> 0% of each run, Pallas kernels for 9% -> 12%
where the time goes in v2:
time: 79.7 us; the launch traced here: 79.6 us
  Pallas kernels  29.3 us (37%)
  starting transfers between devices  23.2 us (29%)
  waiting for transfers between devices  19.9 us (25%)
  matrix products  6.9 us (9%)
    ppermute x19, starting transfers between devices, shifted(): return lax.ppermute(value, axis, pairs)  23.2 us
    ppermute x19, waiting for transfers between devices, shifted(): return lax.ppermute(value, axis, pairs)  19.9 us
    pallas_call x1, Pallas kernels, whitened_spectra(): pl.pallas_call(functools.partial(fir_kernel, windows=windows), in_specs=[...  9.93 us
    dot_general x1, matrix products, dot(): return jnp.dot(a, b, preferred_element_type=jnp.float32)  6.9 us
    pallas_call x2, Pallas kernels, crossed(): pl.pallas_call(functools.partial(cross_kernel, fetch=fetch, own=own, size...  6.29 us
    pallas_call x1, Pallas kernels, correlations(): pl.pallas_call(functools.partial(lag_kernel, scale=1.0 / math.sqrt(NFREQ...  4.8 us
    pallas_call x1, Pallas kernels, expanded_local(): pl.pallas_call(functools.partial(expand_kernel, sizes=sizes), out_shape=j...  3.71 us
    pallas_call x1, Pallas kernels, lag_parts(): pl.pallas_call(functools.partial(part_kernel, sizes=sizes, by_y=by_y), ou...  2.91 us
  transfers between devices with their start and end apart: 19, of which 10 were waited for; matrix products, arithmetic and copies ran while one was open for 0% of the time, Pallas kernels for 12%

profile of v2, /device:TPU:0, one launch (start us, length us, event | category | flops | bytes accessed | tf_op | source)
XLA Modules:
  0.0 79.6 jit_solution(14461739026803746167)
XLA Ops:
  0.0 9.9 %fir.1 = (bf16[8,192,1536]{2,1,0:T(8,128)(2,1)}, bf16[192,16384]{1,0:T(8,128)(2,1)}) custom-call(bf16[192,16384]{1,0:T(8,128)(2,1)} %bitcast.13, bf16[1,32]{1,0:T(2,128)(2,1)} %bitcast.14), custom_call_target="tpu_custom_call" | custom-call | tf_op jit(solution)/shard_map/fir/pallas_call | solution.py:228
  10.0 6.9 %fusion.part_ref = f32[8,192,1024]{2,1,0:T(8,128)S(1)} fusion(bf16[8,192,1536]{2,1,0:T(8,128)(2,1)} %get-tuple-element.30, bf16[1536,1024,1]{1,0,2:T(8,128)(2,1)S(1)} %copy-done.2), kind=kOutput, calls=%fused_computation.1 | convolution fusion | flops 4831838208 | bytes 14155776 | tf_op jit(solution)/shard_map/dot_general | solution.py:48
  16.9 1.3 %whiten.1 = (bf16[2,192,128]{2,1,0:T(8,128)(2,1)S(1)}, bf16[2,192,128]{2,1,0:T(8,128)(2,1)S(1)}, bf16[2,192,128]{2,1,0:T(8,128)(2,1)S(1)}, bf16[2,192,128]{2,1,0...) custom-call(f32[8,192,1024]{2,1,0:T(8,128)S(1)} %fusion.part_ref), custom_call_target="tpu_custom_call" | custom-call | tf_op jit(solution)/shard_map/whiten/pallas_call | solution.py:245
  18.2 3.1 %collective-permute-start = (bf16[2,192,128]{2,1,0:T(8,128)(2,1)S(1)}, bf16[2,192,128]{2,1,0:T(8,128)(2,1)S(1)}, u32[]{:S(2)}, u32[]{:S(2)}) collective-permute-start(bf16[2,192,128]{2,1,0:T(8,128)(2,1)S(1)} %get-tuple-element.32), channel_id=1, source_target_pairs={{0,2},{1,3},{2,4},{3,5},{4,6},{5,7},{6,0},{7,1},{8,10},{9,11},{10,... | collective-permute-start | bytes 294920 | tf_op jit(solution)/shard_map/ppermute | solution.py:104
  21.3 2.6 %collective-permute-start.1 = (bf16[2,192,128]{2,1,0:T(8,128)(2,1)S(1)}, bf16[2,192,128]{2,1,0:T(8,128)(2,1)S(1)}, u32[]{:S(2)}, u32[]{:S(2)}) collective-permute-start(bf16[2,192,128]{2,1,0:T(8,128)(2,1)S(1)} %get-tuple-element.33), channel_id=1, source_target_pairs={{0,4},{1,5},{2,6},{3,7},{4,0},{5,1},{6,2},{7,3},{8,12},{9,13},{10,... | collective-permute-start | bytes 294920 | tf_op jit(solution)/shard_map/ppermute | solution.py:104
  23.9 1.4 %collective-permute-start.2 = (bf16[2,192,128]{2,1,0:T(8,128)(2,1)S(1)}, bf16[2,192,128]{2,1,0:T(8,128)(2,1)S(1)}, u32[]{:S(2)}, u32[]{:S(2)}) collective-permute-start(bf16[2,192,128]{2,1,0:T(8,128)(2,1)S(1)} %get-tuple-element.34), channel_id=1, source_target_pairs={{0,6},{1,7},{2,0},{3,1},{4,2},{5,3},{6,4},{7,5},{8,14},{9,15},{10,... | collective-permute-start | bytes 294920 | tf_op jit(solution)/shard_map/ppermute | solution.py:104
  25.3 1.5 %collective-permute-start.4 = (bf16[3,16,1024]{2,1,0:T(8,128)(2,1)S(1)}, bf16[3,16,1024]{2,1,0:T(8,128)(2,1)S(1)}, u32[]{:S(2)}, u32[]{:S(2)}) collective-permute-start(bf16[3,16,1024]{2,1,0:T(8,128)(2,1)S(1)} %get-tuple-element.37), channel_id=1, source_target_pairs={{0,16},{8,24},{16,0},{24,8},{1,17},{9,25},{17,1},{25,9},{2,18},{10... | collective-permute-start | bytes 294920 | tf_op jit(solution)/shard_map/ppermute | solution.py:104
  27.1 3.4 %collective-permute-done.1.refs_2_ = bf16[2,192,128]{2,1,0:T(8,128)(2,1)S(1)} collective-permute-done((bf16[2,192,128]{2,1,0:T(8,128)(2,1)S(1)}, bf16[2,192,128]{2,1,0:T(8,128)(2,1)S(1)}, u32[]{:S(2)}, u32[]{:S(2)}) %collective-permute-start.1) | collective-permute-done | bytes 98336 | tf_op jit(solution)/shard_map/ppermute | solution.py:104
  30.8 1.3 %collective-permute-done.5.refs_3_ = bf16[3,16,1024]{2,1,0:T(8,128)(2,1)S(1)} collective-permute-done((bf16[3,16,1024]{2,1,0:T(8,128)(2,1)S(1)}, bf16[3,16,1024]{2,1,0:T(8,128)(2,1)S(1)}, u32[]{:S(2)}, u32[]{:S(2)}) %collective-permute-start.5) | collective-permute-done | bytes 98336 | tf_op jit(solution)/shard_map/ppermute | solution.py:104
  32.5 1.6 %collective-permute-start.6 = (bf16[1,3,128,128]{3,2,1,0:T(8,128)(2,1)S(1)}, bf16[1,3,128,128]{3,2,1,0:T(8,128)(2,1)S(1)}, u32[]{:S(2)}, u32[]{:S(2)}) collective-permute-start(bf16[1,3,128,128]{3,2,1,0:T(8,128)(2,1)S(1)} %get-tuple-element.44), channel_id=1, source_target_pairs={{0,1},{1,0},{2,3},{3,2},{4,5},{5,4},{6,7},{7,6},{8,9},{9,8},{10,11... | collective-permute-start | bytes 294920 | tf_op jit(solution)/shard_map/ppermute | solution.py:104
  34.1 3.4 %collective-permute-done.6 = bf16[1,3,128,128]{3,2,1,0:T(8,128)(2,1)S(1)} collective-permute-done((bf16[1,3,128,128]{3,2,1,0:T(8,128)(2,1)S(1)}, bf16[1,3,128,128]{3,2,1,0:T(8,128)(2,1)S(1)}, u32[]{:S(2)}, u32[]{:S(2)}) %collective-permute-start.6) | collective-permute-done | bytes 98336 | tf_op jit(solution)/shard_map/ppermute | solution.py:104
  37.5 1.7 %collective-permute-start.9 = (bf16[1,3,128,128]{3,2,1,0:T(8,128)(2,1)S(1)}, bf16[1,3,128,128]{3,2,1,0:T(8,128)(2,1)S(1)}, u32[]{:S(2)}, u32[]{:S(2)}) collective-permute-start(bf16[1,3,128,128]{3,2,1,0:T(8,128)(2,1)S(1)} %add.3), channel_id=1, source_target_pairs={{0,6},{1,7},{2,0},{3,1},{4,2},{5,3},{6,4},{7,5},{8,14},{9,15},{10,... | collective-permute-start | bytes 294920 | tf_op jit(solution)/shard_map/ppermute | solution.py:104
  39.2 3.3 %collective-permute-start.8 = (bf16[1,3,128,128]{3,2,1,0:T(8,128)(2,1)S(1)}, bf16[1,3,128,128]{3,2,1,0:T(8,128)(2,1)S(1)}, u32[]{:S(2)}, u32[]{:S(2)}) collective-permute-start(bf16[1,3,128,128]{3,2,1,0:T(8,128)(2,1)S(1)} %add.3), channel_id=1, source_target_pairs={{0,4},{1,5},{2,6},{3,7},{4,0},{5,1},{6,2},{7,3},{8,12},{9,13},{10,... | collective-permute-start | bytes 294920 | tf_op jit(solution)/shard_map/ppermute | solution.py:104
  42.6 1.9 %collective-permute-start.7 = (bf16[1,3,128,128]{3,2,1,0:T(8,128)(2,1)S(1)}, bf16[1,3,128,128]{3,2,1,0:T(8,128)(2,1)S(1)}, u32[]{:S(2)}, u32[]{:S(2)}) collective-permute-start(bf16[1,3,128,128]{3,2,1,0:T(8,128)(2,1)S(1)} %add.3), channel_id=1, source_target_pairs={{0,2},{1,3},{2,4},{3,5},{4,6},{5,7},{6,0},{7,1},{8,10},{9,11},{10,... | collective-permute-start | bytes 294920 | tf_op jit(solution)/shard_map/ppermute | solution.py:104
  44.5 6.5 %collective-permute-done.8 = bf16[1,3,128,128]{3,2,1,0:T(8,128)(2,1)S(1)} collective-permute-done((bf16[1,3,128,128]{3,2,1,0:T(8,128)(2,1)S(1)}, bf16[1,3,128,128]{3,2,1,0:T(8,128)(2,1)S(1)}, u32[]{:S(2)}, u32[]{:S(2)}) %collective-permute-start.8) | collective-permute-done | bytes 98336 | tf_op jit(solution)/shard_map/ppermute | solution.py:104
  51.2 1.6 %collective-permute-start.10 = (bf16[4,3,128,128]{3,2,1,0:T(8,128)(2,1)S(1)}, bf16[4,3,128,128]{3,2,1,0:T(8,128)(2,1)S(1)}, u32[]{:S(2)}, u32[]{:S(2)}) collective-permute-start(bf16[4,3,128,128]{3,2,1,0:T(8,128)(2,1)S(1)} %pad_maximum_fusion.refs_0_), channel_id=1, source_target_pairs={{0,1},{1,0},{2,3},{3,2},{4,5},{5,4},{6,7},{7,6},{8,9},{9,8},{10,11... | collective-permute-start | bytes 1179656 | tf_op jit(solution)/shard_map/ppermute | solution.py:104
  52.8 3.7 %expand.1 = bf16[64,16,16,192]{3,2,1,0:T(8,128)(2,1)S(1)} custom-call(bf16[3,16,1024]{2,1,0:T(8,128)(2,1)S(1)} %get-tuple-element.45.refs_0_, bf16[3,16,1024]{2,1,0:T(8,128)(2,1)S(1)} %collective-permute-done.3.refs_1_, bf16[3,16,1024]{2,1,0:T(8,128)(2,1)S(1)} %collective-permute-done.4.refs_2_, bf16[3,16,1024]{2,1,0:T(8,128)(2,1)S(1)} %collective-permute-done.5.refs_3_), custom_call_target="tpu_custom_call" | custom-call | flops 4000000000 | bytes 8388608 | tf_op jit(solution)/shard_map/expand/pallas_call | solution.py:336
  56.6 2.8 %collective-permute-done.11.refs_2_ = bf16[4,3,128,128]{3,2,1,0:T(8,128)(2,1)S(1)} collective-permute-done((bf16[4,3,128,128]{3,2,1,0:T(8,128)(2,1)S(1)}, bf16[4,3,128,128]{3,2,1,0:T(8,128)(2,1)S(1)}, u32[]{:S(2)}, u32[]{:S(2)}) %collective-permute-start.11) | collective-permute-done | bytes 393248 | tf_op jit(solution)/shard_map/ppermute | solution.py:104
  60.0 1.5 %collective-permute-start.14 = (bf16[4,3,64,128]{3,2,1,0:T(8,128)(2,1)S(1)}, bf16[4,3,64,128]{3,2,1,0:T(8,128)(2,1)S(1)}, u32[]{:S(2)}, u32[]{:S(2)}) collective-permute-start(bf16[4,3,64,128]{3,2,1,0:T(8,128)(2,1)S(1)} %slice.7), channel_id=1, source_target_pairs={{0,1},{1,0},{2,3},{3,2},{4,5},{5,4},{6,7},{7,6},{8,9},{9,8},{10,11... | collective-permute-start | bytes 589832 | tf_op jit(solution)/shard_map/ppermute | solution.py:104
  61.6 1.7 %collective-permute-start.13 = (bf16[4,3,64,128]{3,2,1,0:T(8,128)(2,1)S(1)}, bf16[4,3,64,128]{3,2,1,0:T(8,128)(2,1)S(1)}, u32[]{:S(2)}, u32[]{:S(2)}) collective-permute-start(bf16[4,3,64,128]{3,2,1,0:T(8,128)(2,1)S(1)} %slice.6), channel_id=1, source_target_pairs={{0,16},{8,24},{16,0},{24,8},{1,17},{9,25},{17,1},{25,9},{2,18},{10... | collective-permute-start | bytes 589832 | tf_op jit(solution)/shard_map/ppermute | solution.py:104
  63.2 3.1 %cross.2.cross_ref = bf16[2048,512]{1,0:T(8,128)(2,1)S(1)} custom-call(bf16[64,256,192]{2,1,0:T(8,128)(2,1)S(1)} %bitcast.11, bf16[4,3,128,128]{3,2,1,0:T(8,128)(2,1)S(1)} %pad_maximum_fusion.refs_0_, bf16[4,3,128,128]{3,2,1,0:T(8,128)(2,1)S(1)} %collective-permute-done.15.refs_1_, bf16[4,3,128,128]{3,2,1,0:T(8,128)(2,1)S(1)} %collective-permute-done.11.refs_2_, ...), custom_call_target="tpu_custom_call" | custom-call | flops 4000000000 | bytes 8388608 | tf_op jit(solution)/shard_map/cross/pallas_call | solution.py:381
  68.7 2.9 %lags_near.1.refs_2_ = f32[2048,1024]{1,0:T(8,128)S(1)} custom-call(bf16[2048,512]{1,0:T(8,128)(2,1)S(1)} %cross.2.cross_ref, bf16[1024,1024]{1,0:T(8,128)(2,1)S(1)} %copy-done), custom_call_target="tpu_custom_call" | custom-call | flops 4000000000 | bytes 8388608 | tf_op jit(solution)/shard_map/lags_near/pallas_call | solution.py:451
  71.6 3.1 %cross.3.refs_0_ = bf16[2048,512]{1,0:T(8,128)(2,1)S(1)} custom-call(bf16[64,256,192]{2,1,0:T(8,128)(2,1)S(1)} %bitcast.12, bf16[4,3,128,128]{3,2,1,0:T(8,128)(2,1)S(1)} %collective-permute-done.10.refs_0_, bf16[4,3,128,128]{3,2,1,0:T(8,128)(2,1)S(1)} %collective-permute-done.12.refs_1_, bf16[4,3,64,128]{3,2,1,0:T(8,128)(2,1)S(1)} %collective-permute-done.13.refs_2_, ...), custom_call_target="tpu_custom_call" | custom-call | flops 4000000000 | bytes 8388608 | tf_op jit(solution)/shard_map/cross/pallas_call | solution.py:381
  74.8 4.8 %lags.1 = f32[2048,1024]{1,0:T(8,128)} custom-call(bf16[2048,512]{1,0:T(8,128)(2,1)S(1)} %cross.3.refs_0_, bf16[1024,1024]{1,0:T(8,128)(2,1)S(1)} %copy-done, f32[2048,1024]{1,0:T(8,128)S(1)} %lags_near.1.refs_2_), custom_call_target="tpu_custom_call" | custom-call | tf_op jit(solution)/shard_map/lags/pallas_call | solution.py:464
  (33 shorter events, 4.3 us)
Async XLA Ops:
  0.0 9.9 %copy-start.2 = (bf16[1536,1024,1]{1,0,2:T(8,128)(2,1)S(1)}, bf16[1536,1024,1]{1,0,2:T(8,128)(2,1)}, u32[]{:S(2)}) copy-start(bf16[1536,1024,1]{1,0,2:T(8,128)(2,1)} %constant.7) | copy-start | bytes 9437188
  16.9 15.3 %copy-start.1 = (s32[128]{0:T(128)S(1)}, s32[128]{0:T(128)}, u32[]{:S(2)}) copy-start(s32[128]{0:T(128)} %param.8) | copy-start | bytes 1540
  18.2 8.8 %collective-permute-start = (bf16[2,192,128]{2,1,0:T(8,128)(2,1)S(1)}, bf16[2,192,128]{2,1,0:T(8,128)(2,1)S(1)}, u32[]{:S(2)}, u32[]{:S(2)}) collective-permute-start(bf16[2,192,128]{2,1,0:T(8,128)(2,1)S(1)} %get-tuple-element.32), channel_id=1, source_target_pairs={{0,2},{1,3},{2,4},{3,5},{4,6},{5,7},{6,0},{7,1},{8,10},{9,11},{10,... | collective-permute-start | bytes 294920 | tf_op jit(solution)/shard_map/ppermute | solution.py:104
  21.3 9.2 %collective-permute-start.1 = (bf16[2,192,128]{2,1,0:T(8,128)(2,1)S(1)}, bf16[2,192,128]{2,1,0:T(8,128)(2,1)S(1)}, u32[]{:S(2)}, u32[]{:S(2)}) collective-permute-start(bf16[2,192,128]{2,1,0:T(8,128)(2,1)S(1)} %get-tuple-element.33), channel_id=1, source_target_pairs={{0,4},{1,5},{2,6},{3,7},{4,0},{5,1},{6,2},{7,3},{8,12},{9,13},{10,... | collective-permute-start | bytes 294920 | tf_op jit(solution)/shard_map/ppermute | solution.py:104
  23.9 6.6 %collective-permute-start.2 = (bf16[2,192,128]{2,1,0:T(8,128)(2,1)S(1)}, bf16[2,192,128]{2,1,0:T(8,128)(2,1)S(1)}, u32[]{:S(2)}, u32[]{:S(2)}) collective-permute-start(bf16[2,192,128]{2,1,0:T(8,128)(2,1)S(1)} %get-tuple-element.34), channel_id=1, source_target_pairs={{0,6},{1,7},{2,0},{3,1},{4,2},{5,3},{6,4},{7,5},{8,14},{9,15},{10,... | collective-permute-start | bytes 294920 | tf_op jit(solution)/shard_map/ppermute | solution.py:104
  25.2 5.3 %collective-permute-start.3 = (bf16[3,16,1024]{2,1,0:T(8,128)(2,1)S(1)}, bf16[3,16,1024]{2,1,0:T(8,128)(2,1)S(1)}, u32[]{:S(2)}, u32[]{:S(2)}) collective-permute-start(bf16[3,16,1024]{2,1,0:T(8,128)(2,1)S(1)} %get-tuple-element.36), channel_id=1, source_target_pairs={{0,8},{8,0},{16,24},{24,16},{1,9},{9,1},{17,25},{25,17},{2,10},{10... | collective-permute-start | bytes 294920 | tf_op jit(solution)/shard_map/ppermute | solution.py:104
  25.3 5.6 %collective-permute-start.4 = (bf16[3,16,1024]{2,1,0:T(8,128)(2,1)S(1)}, bf16[3,16,1024]{2,1,0:T(8,128)(2,1)S(1)}, u32[]{:S(2)}, u32[]{:S(2)}) collective-permute-start(bf16[3,16,1024]{2,1,0:T(8,128)(2,1)S(1)} %get-tuple-element.37), channel_id=1, source_target_pairs={{0,16},{8,24},{16,0},{24,8},{1,17},{9,25},{17,1},{25,9},{2,18},{10... | collective-permute-start | bytes 294920 | tf_op jit(solution)/shard_map/ppermute | solution.py:104
  27.0 5.2 %collective-permute-start.5 = (bf16[3,16,1024]{2,1,0:T(8,128)(2,1)S(1)}, bf16[3,16,1024]{2,1,0:T(8,128)(2,1)S(1)}, u32[]{:S(2)}, u32[]{:S(2)}) collective-permute-start(bf16[3,16,1024]{2,1,0:T(8,128)(2,1)S(1)} %get-tuple-element.38), channel_id=1, source_target_pairs={{0,24},{8,16},{16,8},{24,0},{1,25},{9,17},{17,9},{25,1},{2,26},{10... | collective-permute-start | bytes 294920 | tf_op jit(solution)/shard_map/ppermute | solution.py:104
  32.5 5.0 %collective-permute-start.6 = (bf16[1,3,128,128]{3,2,1,0:T(8,128)(2,1)S(1)}, bf16[1,3,128,128]{3,2,1,0:T(8,128)(2,1)S(1)}, u32[]{:S(2)}, u32[]{:S(2)}) collective-permute-start(bf16[1,3,128,128]{3,2,1,0:T(8,128)(2,1)S(1)} %get-tuple-element.44), channel_id=1, source_target_pairs={{0,1},{1,0},{2,3},{3,2},{4,5},{5,4},{6,7},{7,6},{8,9},{9,8},{10,11... | collective-permute-start | bytes 294920 | tf_op jit(solution)/shard_map/ppermute | solution.py:104
  37.5 7.0 %collective-permute-start.9 = (bf16[1,3,128,128]{3,2,1,0:T(8,128)(2,1)S(1)}, bf16[1,3,128,128]{3,2,1,0:T(8,128)(2,1)S(1)}, u32[]{:S(2)}, u32[]{:S(2)}) collective-permute-start(bf16[1,3,128,128]{3,2,1,0:T(8,128)(2,1)S(1)} %add.3), channel_id=1, source_target_pairs={{0,6},{1,7},{2,0},{3,1},{4,2},{5,3},{6,4},{7,5},{8,14},{9,15},{10,... | collective-permute-start | bytes 294920 | tf_op jit(solution)/shard_map/ppermute | solution.py:104
  39.2 11.8 %collective-permute-start.8 = (bf16[1,3,128,128]{3,2,1,0:T(8,128)(2,1)S(1)}, bf16[1,3,128,128]{3,2,1,0:T(8,128)(2,1)S(1)}, u32[]{:S(2)}, u32[]{:S(2)}) collective-permute-start(bf16[1,3,128,128]{3,2,1,0:T(8,128)(2,1)S(1)} %add.3), channel_id=1, source_target_pairs={{0,4},{1,5},{2,6},{3,7},{4,0},{5,1},{6,2},{7,3},{8,12},{9,13},{10,... | collective-permute-start | bytes 294920 | tf_op jit(solution)/shard_map/ppermute | solution.py:104
  42.6 8.5 %collective-permute-start.7 = (bf16[1,3,128,128]{3,2,1,0:T(8,128)(2,1)S(1)}, bf16[1,3,128,128]{3,2,1,0:T(8,128)(2,1)S(1)}, u32[]{:S(2)}, u32[]{:S(2)}) collective-permute-start(bf16[1,3,128,128]{3,2,1,0:T(8,128)(2,1)S(1)} %add.3), channel_id=1, source_target_pairs={{0,2},{1,3},{2,4},{3,5},{4,6},{5,7},{6,0},{7,1},{8,10},{9,11},{10,... | collective-permute-start | bytes 294920 | tf_op jit(solution)/shard_map/ppermute | solution.py:104
  51.1 8.2 %collective-permute-start.11 = (bf16[4,3,128,128]{3,2,1,0:T(8,128)(2,1)S(1)}, bf16[4,3,128,128]{3,2,1,0:T(8,128)(2,1)S(1)}, u32[]{:S(2)}, u32[]{:S(2)}) collective-permute-start(bf16[4,3,128,128]{3,2,1,0:T(8,128)(2,1)S(1)} %pad_maximum_fusion.refs_0_), channel_id=1, source_target_pairs={{0,16},{8,24},{16,0},{24,8},{1,17},{9,25},{17,1},{25,9},{2,18},{10... | collective-permute-start | bytes 1179656 | tf_op jit(solution)/shard_map/ppermute | solution.py:104
  51.2 8.2 %collective-permute-start.10 = (bf16[4,3,128,128]{3,2,1,0:T(8,128)(2,1)S(1)}, bf16[4,3,128,128]{3,2,1,0:T(8,128)(2,1)S(1)}, u32[]{:S(2)}, u32[]{:S(2)}) collective-permute-start(bf16[4,3,128,128]{3,2,1,0:T(8,128)(2,1)S(1)} %pad_maximum_fusion.refs_0_), channel_id=1, source_target_pairs={{0,1},{1,0},{2,3},{3,2},{4,5},{5,4},{6,7},{7,6},{8,9},{9,8},{10,11... | collective-permute-start | bytes 1179656 | tf_op jit(solution)/shard_map/ppermute | solution.py:104
  56.5 6.7 %collective-permute-start.15 = (bf16[4,3,128,128]{3,2,1,0:T(8,128)(2,1)S(1)}, bf16[4,3,128,128]{3,2,1,0:T(8,128)(2,1)S(1)}, u32[]{:S(2)}, u32[]{:S(2)}) collective-permute-start(bf16[4,3,128,128]{3,2,1,0:T(8,128)(2,1)S(1)} %pad_maximum_fusion.refs_0_), channel_id=1, source_target_pairs={{0,8},{8,0},{16,24},{24,16},{1,9},{9,1},{17,25},{25,17},{2,10},{10... | collective-permute-start | bytes 1179656 | tf_op jit(solution)/shard_map/ppermute | solution.py:104
  59.4 3.8 %collective-permute-start.16 = (bf16[4,3,128,128]{3,2,1,0:T(8,128)(2,1)S(1)}, bf16[4,3,128,128]{3,2,1,0:T(8,128)(2,1)S(1)}, u32[]{:S(2)}, u32[]{:S(2)}) collective-permute-start(bf16[4,3,128,128]{3,2,1,0:T(8,128)(2,1)S(1)} %collective-permute-done.11.refs_2_), channel_id=1, source_target_pairs={{0,8},{8,0},{16,24},{24,16},{1,9},{9,1},{17,25},{25,17},{2,10},{10... | collective-permute-start | bytes 1179656 | tf_op jit(solution)/shard_map/ppermute | solution.py:104
  59.5 9.2 %copy-start = (bf16[1024,1024]{1,0:T(8,128)(2,1)S(1)}, bf16[1024,1024]{1,0:T(8,128)(2,1)}, u32[]{:S(2)}) copy-start(bf16[1024,1024]{1,0:T(8,128)(2,1)} %constant.5.clone.table_ref.refs_1_) | copy-start | bytes 6291460
  59.5 12.1 %collective-permute-start.12 = (bf16[4,3,128,128]{3,2,1,0:T(8,128)(2,1)S(1)}, bf16[4,3,128,128]{3,2,1,0:T(8,128)(2,1)S(1)}, u32[]{:S(2)}, u32[]{:S(2)}) collective-permute-start(bf16[4,3,128,128]{3,2,1,0:T(8,128)(2,1)S(1)} %collective-permute-done.10.refs_0_), channel_id=1, source_target_pairs={{0,8},{8,0},{16,24},{24,16},{1,9},{9,1},{17,25},{25,17},{2,10},{10... | collective-permute-start | bytes 1179656 | tf_op jit(solution)/shard_map/ppermute | solution.py:104
  60.0 6.9 %collective-permute-start.14 = (bf16[4,3,64,128]{3,2,1,0:T(8,128)(2,1)S(1)}, bf16[4,3,64,128]{3,2,1,0:T(8,128)(2,1)S(1)}, u32[]{:S(2)}, u32[]{:S(2)}) collective-permute-start(bf16[4,3,64,128]{3,2,1,0:T(8,128)(2,1)S(1)} %slice.7), channel_id=1, source_target_pairs={{0,1},{1,0},{2,3},{3,2},{4,5},{5,4},{6,7},{7,6},{8,9},{9,8},{10,11... | collective-permute-start | bytes 589832 | tf_op jit(solution)/shard_map/ppermute | solution.py:104
  61.6 6.6 %collective-permute-start.13 = (bf16[4,3,64,128]{3,2,1,0:T(8,128)(2,1)S(1)}, bf16[4,3,64,128]{3,2,1,0:T(8,128)(2,1)S(1)}, u32[]{:S(2)}, u32[]{:S(2)}) collective-permute-start(bf16[4,3,64,128]{3,2,1,0:T(8,128)(2,1)S(1)} %slice.6), channel_id=1, source_target_pairs={{0,16},{8,24},{16,0},{24,8},{1,17},{9,25},{17,1},{25,9},{2,18},{10... | collective-permute-start | bytes 589832 | tf_op jit(solution)/shard_map/ppermute | solution.py:104
  68.2 3.4 %collective-permute-start.17 = (bf16[4,3,64,128]{3,2,1,0:T(8,128)(2,1)S(1)}, bf16[4,3,64,128]{3,2,1,0:T(8,128)(2,1)S(1)}, u32[]{:S(2)}, u32[]{:S(2)}) collective-permute-start(bf16[4,3,64,128]{3,2,1,0:T(8,128)(2,1)S(1)} %collective-permute-done.13.refs_2_), channel_id=1, source_target_pairs={{0,8},{8,0},{16,24},{24,16},{1,9},{9,1},{17,25},{25,17},{2,10},{10... | collective-permute-start | bytes 589832 | tf_op jit(solution)/shard_map/ppermute | solution.py:104
  68.2 3.5 %collective-permute-start.18 = (bf16[4,3,64,128]{3,2,1,0:T(8,128)(2,1)S(1)}, bf16[4,3,64,128]{3,2,1,0:T(8,128)(2,1)S(1)}, u32[]{:S(2)}, u32[]{:S(2)}) collective-permute-start(bf16[4,3,64,128]{3,2,1,0:T(8,128)(2,1)S(1)} %collective-permute-done.14.refs_3_), channel_id=1, source_target_pairs={{0,8},{8,0},{16,24},{24,16},{1,9},{9,1},{17,25},{25,17},{2,10},{10... | collective-permute-start | bytes 589832 | tf_op jit(solution)/shard_map/ppermute | solution.py:104

commit v3 on v2

--- a/solution.py
+++ b/solution.py
@@ -225,20 +225,17 @@
     own = chans // tm_count
     x = jnp.transpose(strain, (1, 0, 2)).reshape(rows, samples)
     blocks = WIN // SUB
-    filtered, _ = pl.pallas_call(
+    filtered = pl.pallas_call(
         functools.partial(fir_kernel, windows=windows),
         in_specs=[pl.BlockSpec(memory_space=pl.ANY)] * 2,
-        out_specs=[pl.BlockSpec(memory_space=pltpu.VMEM)] * 2,
-        out_shape=[
-            jax.ShapeDtypeStruct((blocks, rows, 3 * SUB), jnp.bfloat16),
-            jax.ShapeDtypeStruct((rows, samples), jnp.bfloat16),
-        ],
+        out_shape=jax.ShapeDtypeStruct((blocks, rows, 3 * SUB), jnp.bfloat16),
         scratch_shapes=[
+            pltpu.VMEM((rows, samples), jnp.bfloat16),
             pltpu.VMEM((1, TAPS), jnp.bfloat16),
             pltpu.VMEM((FIR_IN, FIR_OUT), jnp.bfloat16),
             pltpu.SemaphoreType.DMA((windows + 1,)),
         ],
-        compiler_params=pltpu.CompilerParams(vmem_limit_bytes=58 * MIB),
+        compiler_params=pltpu.CompilerParams(vmem_limit_bytes=46 * MIB),
         name="fir",
     )(x, taps.reshape(1, TAPS))
     part = dot(filtered.reshape(blocks * rows, 3 * SUB), jnp.asarray(forward_constants()))

time: 79.7 us -> 75 us (0.941)
  Pallas kernels: 29.3 us -> 25.3 us
  matrix products: 6.9 us -> 5.34 us
    pallas_call x1, Pallas kernels: 9.93 us -> 5.9 us  [whitened_spectra(): pl.pallas_call(functools.partial(fir_kernel, windows=windows), in_specs=[...]
    dot_general x1, matrix products: 6.9 us -> 5.34 us  [dot(): return jnp.dot(a, b, preferred_element_type=jnp.float32)]
  transfers between devices with their start and end apart: 19 -> 19, of which waited for: 10 -> 10; matrix products, arithmetic and copies ran while one was open for 0% -> 0% of each run, Pallas kernels for 12% -> 13%
where the time goes in v3:
time: 75 us; the launch traced here: 74.8 us
  Pallas kernels  25.3 us (34%)
  starting transfers between devices  23.2 us (31%)
  waiting for transfers between devices  19.9 us (27%)
  matrix products  5.34 us (7%)
    ppermute x19, starting transfers between devices, shifted(): return lax.ppermute(value, axis, pairs)  23.2 us
    ppermute x19, waiting for transfers between devices, shifted(): return lax.ppermute(value, axis, pairs)  19.9 us
    pallas_call x2, Pallas kernels, crossed(): pl.pallas_call(functools.partial(cross_kernel, fetch=fetch, own=own, size...  6.31 us
    pallas_call x1, Pallas kernels, whitened_spectra(): pl.pallas_call(functools.partial(fir_kernel, windows=windows), in_specs=[...  5.9 us
    dot_general x1, matrix products, dot(): return jnp.dot(a, b, preferred_element_type=jnp.float32)  5.34 us
    pallas_call x1, Pallas kernels, correlations(): pl.pallas_call(functools.partial(lag_kernel, scale=1.0 / math.sqrt(NFREQ...  4.8 us
    pallas_call x1, Pallas kernels, expanded_local(): pl.pallas_call(functools.partial(expand_kernel, sizes=sizes), out_shape=j...  3.71 us
    pallas_call x1, Pallas kernels, lag_parts(): pl.pallas_call(functools.partial(part_kernel, sizes=sizes, by_y=by_y), ou...  2.91 us
  transfers between devices with their start and end apart: 19, of which 10 were waited for; matrix products, arithmetic and copies ran while one was open for 0% of the time, Pallas kernels for 13%

profile of v3, /device:TPU:0, one launch (start us, length us, event | category | flops | bytes accessed | tf_op | source)
XLA Modules:
  0.0 74.8 jit_solution(13216681184788521331)
XLA Ops:
  0.7 5.9 %fir.1 = bf16[8,192,1536]{2,1,0:T(8,128)(2,1)S(1)} custom-call(bf16[192,16384]{1,0:T(8,128)(2,1)} %bitcast.14, bf16[1,32]{1,0:T(2,128)(2,1)S(1)} %bitcast.10), custom_call_target="tpu_custom_call" | custom-call | tf_op jit(solution)/shard_map/fir/pallas_call | solution.py:228
  6.6 5.3 %fusion.part_ref = f32[8,192,1024]{2,1,0:T(8,128)S(1)} fusion(bf16[8,192,1536]{2,1,0:T(8,128)(2,1)S(1)} %fir.1, bf16[1536,1024,1]{1,0,2:T(8,128)(2,1)S(1)} %copy-done.3), kind=kOutput, calls=%fused_computation.1 | convolution fusion | flops 4831838208 | bytes 14155776 | tf_op jit(solution)/shard_map/dot_general | solution.py:48
  11.9 1.3 %whiten.1 = (bf16[2,192,128]{2,1,0:T(8,128)(2,1)S(1)}, bf16[2,192,128]{2,1,0:T(8,128)(2,1)S(1)}, bf16[2,192,128]{2,1,0:T(8,128)(2,1)S(1)}, bf16[2,192,128]{2,1,0...) custom-call(f32[8,192,1024]{2,1,0:T(8,128)S(1)} %fusion.part_ref), custom_call_target="tpu_custom_call" | custom-call | tf_op jit(solution)/shard_map/whiten/pallas_call | solution.py:242
  13.3 3.1 %collective-permute-start = (bf16[2,192,128]{2,1,0:T(8,128)(2,1)S(1)}, bf16[2,192,128]{2,1,0:T(8,128)(2,1)S(1)}, u32[]{:S(2)}, u32[]{:S(2)}) collective-permute-start(bf16[2,192,128]{2,1,0:T(8,128)(2,1)S(1)} %get-tuple-element.30), channel_id=1, source_target_pairs={{0,2},{1,3},{2,4},{3,5},{4,6},{5,7},{6,0},{7,1},{8,10},{9,11},{10,... | collective-permute-start | bytes 294920 | tf_op jit(solution)/shard_map/ppermute | solution.py:104
  16.4 2.6 %collective-permute-start.1 = (bf16[2,192,128]{2,1,0:T(8,128)(2,1)S(1)}, bf16[2,192,128]{2,1,0:T(8,128)(2,1)S(1)}, u32[]{:S(2)}, u32[]{:S(2)}) collective-permute-start(bf16[2,192,128]{2,1,0:T(8,128)(2,1)S(1)} %get-tuple-element.31), channel_id=1, source_target_pairs={{0,4},{1,5},{2,6},{3,7},{4,0},{5,1},{6,2},{7,3},{8,12},{9,13},{10,... | collective-permute-start | bytes 294920 | tf_op jit(solution)/shard_map/ppermute | solution.py:104
  19.0 1.3 %collective-permute-start.2 = (bf16[2,192,128]{2,1,0:T(8,128)(2,1)S(1)}, bf16[2,192,128]{2,1,0:T(8,128)(2,1)S(1)}, u32[]{:S(2)}, u32[]{:S(2)}) collective-permute-start(bf16[2,192,128]{2,1,0:T(8,128)(2,1)S(1)} %get-tuple-element.32), channel_id=1, source_target_pairs={{0,6},{1,7},{2,0},{3,1},{4,2},{5,3},{6,4},{7,5},{8,14},{9,15},{10,... | collective-permute-start | bytes 294920 | tf_op jit(solution)/shard_map/ppermute | solution.py:104
  20.3 1.5 %collective-permute-start.4 = (bf16[3,16,1024]{2,1,0:T(8,128)(2,1)S(1)}, bf16[3,16,1024]{2,1,0:T(8,128)(2,1)S(1)}, u32[]{:S(2)}, u32[]{:S(2)}) collective-permute-start(bf16[3,16,1024]{2,1,0:T(8,128)(2,1)S(1)} %get-tuple-element.35), channel_id=1, source_target_pairs={{0,16},{8,24},{16,0},{24,8},{1,17},{9,25},{17,1},{25,9},{2,18},{10... | collective-permute-start | bytes 294920 | tf_op jit(solution)/shard_map/ppermute | solution.py:104
  22.2 3.4 %collective-permute-done.1.refs_2_ = bf16[2,192,128]{2,1,0:T(8,128)(2,1)S(1)} collective-permute-done((bf16[2,192,128]{2,1,0:T(8,128)(2,1)S(1)}, bf16[2,192,128]{2,1,0:T(8,128)(2,1)S(1)}, u32[]{:S(2)}, u32[]{:S(2)}) %collective-permute-start.1) | collective-permute-done | bytes 98336 | tf_op jit(solution)/shard_map/ppermute | solution.py:104
  25.9 1.3 %collective-permute-done.5.refs_3_ = bf16[3,16,1024]{2,1,0:T(8,128)(2,1)S(1)} collective-permute-done((bf16[3,16,1024]{2,1,0:T(8,128)(2,1)S(1)}, bf16[3,16,1024]{2,1,0:T(8,128)(2,1)S(1)}, u32[]{:S(2)}, u32[]{:S(2)}) %collective-permute-start.5) | collective-permute-done | bytes 98336 | tf_op jit(solution)/shard_map/ppermute | solution.py:104
  27.5 1.6 %collective-permute-start.6 = (bf16[1,3,128,128]{3,2,1,0:T(8,128)(2,1)S(1)}, bf16[1,3,128,128]{3,2,1,0:T(8,128)(2,1)S(1)}, u32[]{:S(2)}, u32[]{:S(2)}) collective-permute-start(bf16[1,3,128,128]{3,2,1,0:T(8,128)(2,1)S(1)} %get-tuple-element.42), channel_id=1, source_target_pairs={{0,1},{1,0},{2,3},{3,2},{4,5},{5,4},{6,7},{7,6},{8,9},{9,8},{10,11... | collective-permute-start | bytes 294920 | tf_op jit(solution)/shard_map/ppermute | solution.py:104
  29.1 3.4 %collective-permute-done.6 = bf16[1,3,128,128]{3,2,1,0:T(8,128)(2,1)S(1)} collective-permute-done((bf16[1,3,128,128]{3,2,1,0:T(8,128)(2,1)S(1)}, bf16[1,3,128,128]{3,2,1,0:T(8,128)(2,1)S(1)}, u32[]{:S(2)}, u32[]{:S(2)}) %collective-permute-start.6) | collective-permute-done | bytes 98336 | tf_op jit(solution)/shard_map/ppermute | solution.py:104
  32.6 1.7 %collective-permute-start.9 = (bf16[1,3,128,128]{3,2,1,0:T(8,128)(2,1)S(1)}, bf16[1,3,128,128]{3,2,1,0:T(8,128)(2,1)S(1)}, u32[]{:S(2)}, u32[]{:S(2)}) collective-permute-start(bf16[1,3,128,128]{3,2,1,0:T(8,128)(2,1)S(1)} %add.3), channel_id=1, source_target_pairs={{0,6},{1,7},{2,0},{3,1},{4,2},{5,3},{6,4},{7,5},{8,14},{9,15},{10,... | collective-permute-start | bytes 294920 | tf_op jit(solution)/shard_map/ppermute | solution.py:104
  34.3 3.3 %collective-permute-start.8 = (bf16[1,3,128,128]{3,2,1,0:T(8,128)(2,1)S(1)}, bf16[1,3,128,128]{3,2,1,0:T(8,128)(2,1)S(1)}, u32[]{:S(2)}, u32[]{:S(2)}) collective-permute-start(bf16[1,3,128,128]{3,2,1,0:T(8,128)(2,1)S(1)} %add.3), channel_id=1, source_target_pairs={{0,4},{1,5},{2,6},{3,7},{4,0},{5,1},{6,2},{7,3},{8,12},{9,13},{10,... | collective-permute-start | bytes 294920 | tf_op jit(solution)/shard_map/ppermute | solution.py:104
  37.6 1.9 %collective-permute-start.7 = (bf16[1,3,128,128]{3,2,1,0:T(8,128)(2,1)S(1)}, bf16[1,3,128,128]{3,2,1,0:T(8,128)(2,1)S(1)}, u32[]{:S(2)}, u32[]{:S(2)}) collective-permute-start(bf16[1,3,128,128]{3,2,1,0:T(8,128)(2,1)S(1)} %add.3), channel_id=1, source_target_pairs={{0,2},{1,3},{2,4},{3,5},{4,6},{5,7},{6,0},{7,1},{8,10},{9,11},{10,... | collective-permute-start | bytes 294920 | tf_op jit(solution)/shard_map/ppermute | solution.py:104
  39.6 6.5 %collective-permute-done.8 = bf16[1,3,128,128]{3,2,1,0:T(8,128)(2,1)S(1)} collective-permute-done((bf16[1,3,128,128]{3,2,1,0:T(8,128)(2,1)S(1)}, bf16[1,3,128,128]{3,2,1,0:T(8,128)(2,1)S(1)}, u32[]{:S(2)}, u32[]{:S(2)}) %collective-permute-start.8) | collective-permute-done | bytes 98336 | tf_op jit(solution)/shard_map/ppermute | solution.py:104
  46.2 1.6 %collective-permute-start.10 = (bf16[4,3,128,128]{3,2,1,0:T(8,128)(2,1)S(1)}, bf16[4,3,128,128]{3,2,1,0:T(8,128)(2,1)S(1)}, u32[]{:S(2)}, u32[]{:S(2)}) collective-permute-start(bf16[4,3,128,128]{3,2,1,0:T(8,128)(2,1)S(1)} %pad_maximum_fusion.refs_0_), channel_id=1, source_target_pairs={{0,1},{1,0},{2,3},{3,2},{4,5},{5,4},{6,7},{7,6},{8,9},{9,8},{10,11... | collective-permute-start | bytes 1179656 | tf_op jit(solution)/shard_map/ppermute | solution.py:104
  47.8 3.7 %expand.1 = bf16[64,16,16,192]{3,2,1,0:T(8,128)(2,1)S(1)} custom-call(bf16[3,16,1024]{2,1,0:T(8,128)(2,1)S(1)} %get-tuple-element.43.refs_0_, bf16[3,16,1024]{2,1,0:T(8,128)(2,1)S(1)} %collective-permute-done.3.refs_1_, bf16[3,16,1024]{2,1,0:T(8,128)(2,1)S(1)} %collective-permute-done.4.refs_2_, bf16[3,16,1024]{2,1,0:T(8,128)(2,1)S(1)} %collective-permute-done.5.refs_3_), custom_call_target="tpu_custom_call" | custom-call | flops 4000000000 | bytes 8388608 | tf_op jit(solution)/shard_map/expand/pallas_call | solution.py:333
  51.6 2.8 %collective-permute-done.11.refs_2_ = bf16[4,3,128,128]{3,2,1,0:T(8,128)(2,1)S(1)} collective-permute-done((bf16[4,3,128,128]{3,2,1,0:T(8,128)(2,1)S(1)}, bf16[4,3,128,128]{3,2,1,0:T(8,128)(2,1)S(1)}, u32[]{:S(2)}, u32[]{:S(2)}) %collective-permute-start.11) | collective-permute-done | bytes 393248 | tf_op jit(solution)/shard_map/ppermute | solution.py:104
  55.1 1.5 %collective-permute-start.14 = (bf16[4,3,64,128]{3,2,1,0:T(8,128)(2,1)S(1)}, bf16[4,3,64,128]{3,2,1,0:T(8,128)(2,1)S(1)}, u32[]{:S(2)}, u32[]{:S(2)}) collective-permute-start(bf16[4,3,64,128]{3,2,1,0:T(8,128)(2,1)S(1)} %slice.7), channel_id=1, source_target_pairs={{0,1},{1,0},{2,3},{3,2},{4,5},{5,4},{6,7},{7,6},{8,9},{9,8},{10,11... | collective-permute-start | bytes 589832 | tf_op jit(solution)/shard_map/ppermute | solution.py:104
  56.6 1.7 %collective-permute-start.13 = (bf16[4,3,64,128]{3,2,1,0:T(8,128)(2,1)S(1)}, bf16[4,3,64,128]{3,2,1,0:T(8,128)(2,1)S(1)}, u32[]{:S(2)}, u32[]{:S(2)}) collective-permute-start(bf16[4,3,64,128]{3,2,1,0:T(8,128)(2,1)S(1)} %slice.6), channel_id=1, source_target_pairs={{0,16},{8,24},{16,0},{24,8},{1,17},{9,25},{17,1},{25,9},{2,18},{10... | collective-permute-start | bytes 589832 | tf_op jit(solution)/shard_map/ppermute | solution.py:104
  58.3 3.1 %cross.2.cross_ref = bf16[2048,512]{1,0:T(8,128)(2,1)S(1)} custom-call(bf16[64,256,192]{2,1,0:T(8,128)(2,1)S(1)} %bitcast.12, bf16[4,3,128,128]{3,2,1,0:T(8,128)(2,1)S(1)} %pad_maximum_fusion.refs_0_, bf16[4,3,128,128]{3,2,1,0:T(8,128)(2,1)S(1)} %collective-permute-done.15.refs_1_, bf16[4,3,128,128]{3,2,1,0:T(8,128)(2,1)S(1)} %collective-permute-done.11.refs_2_, ...), custom_call_target="tpu_custom_call" | custom-call | flops 4000000000 | bytes 8388608 | tf_op jit(solution)/shard_map/cross/pallas_call | solution.py:378
  63.7 2.9 %lags_near.1.refs_2_ = f32[2048,1024]{1,0:T(8,128)S(1)} custom-call(bf16[2048,512]{1,0:T(8,128)(2,1)S(1)} %cross.2.cross_ref, bf16[1024,1024]{1,0:T(8,128)(2,1)S(1)} %copy-done), custom_call_target="tpu_custom_call" | custom-call | flops 4000000000 | bytes 8388608 | tf_op jit(solution)/shard_map/lags_near/pallas_call | solution.py:448
  66.7 3.2 %cross.3.refs_0_ = bf16[2048,512]{1,0:T(8,128)(2,1)S(1)} custom-call(bf16[64,256,192]{2,1,0:T(8,128)(2,1)S(1)} %bitcast.13, bf16[4,3,128,128]{3,2,1,0:T(8,128)(2,1)S(1)} %collective-permute-done.10.refs_0_, bf16[4,3,128,128]{3,2,1,0:T(8,128)(2,1)S(1)} %collective-permute-done.12.refs_1_, bf16[4,3,64,128]{3,2,1,0:T(8,128)(2,1)S(1)} %collective-permute-done.13.refs_2_, ...), custom_call_target="tpu_custom_call" | custom-call | flops 4000000000 | bytes 8388608 | tf_op jit(solution)/shard_map/cross/pallas_call | solution.py:378
  69.9 4.8 %lags.1 = f32[2048,1024]{1,0:T(8,128)} custom-call(bf16[2048,512]{1,0:T(8,128)(2,1)S(1)} %cross.3.refs_0_, bf16[1024,1024]{1,0:T(8,128)(2,1)S(1)} %copy-done, f32[2048,1024]{1,0:T(8,128)S(1)} %lags_near.1.refs_2_), custom_call_target="tpu_custom_call" | custom-call | tf_op jit(solution)/shard_map/lags/pallas_call | solution.py:461
  (35 shorter events, 4.9 us)
Async XLA Ops:
  0.0 0.7 copy-start.1
  0.7 5.9 %copy-start.3 = (bf16[1536,1024,1]{1,0,2:T(8,128)(2,1)S(1)}, bf16[1536,1024,1]{1,0,2:T(8,128)(2,1)}, u32[]{:S(2)}) copy-start(bf16[1536,1024,1]{1,0,2:T(8,128)(2,1)} %constant.7) | copy-start | bytes 9437188
  11.9 15.3 %copy-start.2 = (s32[128]{0:T(128)S(1)}, s32[128]{0:T(128)}, u32[]{:S(2)}) copy-start(s32[128]{0:T(128)} %param.8) | copy-start | bytes 1540
  13.3 8.8 %collective-permute-start = (bf16[2,192,128]{2,1,0:T(8,128)(2,1)S(1)}, bf16[2,192,128]{2,1,0:T(8,128)(2,1)S(1)}, u32[]{:S(2)}, u32[]{:S(2)}) collective-permute-start(bf16[2,192,128]{2,1,0:T(8,128)(2,1)S(1)} %get-tuple-element.30), channel_id=1, source_target_pairs={{0,2},{1,3},{2,4},{3,5},{4,6},{5,7},{6,0},{7,1},{8,10},{9,11},{10,... | collective-permute-start | bytes 294920 | tf_op jit(solution)/shard_map/ppermute | solution.py:104
  16.4 9.2 %collective-permute-start.1 = (bf16[2,192,128]{2,1,0:T(8,128)(2,1)S(1)}, bf16[2,192,128]{2,1,0:T(8,128)(2,1)S(1)}, u32[]{:S(2)}, u32[]{:S(2)}) collective-permute-start(bf16[2,192,128]{2,1,0:T(8,128)(2,1)S(1)} %get-tuple-element.31), channel_id=1, source_target_pairs={{0,4},{1,5},{2,6},{3,7},{4,0},{5,1},{6,2},{7,3},{8,12},{9,13},{10,... | collective-permute-start | bytes 294920 | tf_op jit(solution)/shard_map/ppermute | solution.py:104
  19.0 6.6 %collective-permute-start.2 = (bf16[2,192,128]{2,1,0:T(8,128)(2,1)S(1)}, bf16[2,192,128]{2,1,0:T(8,128)(2,1)S(1)}, u32[]{:S(2)}, u32[]{:S(2)}) collective-permute-start(bf16[2,192,128]{2,1,0:T(8,128)(2,1)S(1)} %get-tuple-element.32), channel_id=1, source_target_pairs={{0,6},{1,7},{2,0},{3,1},{4,2},{5,3},{6,4},{7,5},{8,14},{9,15},{10,... | collective-permute-start | bytes 294920 | tf_op jit(solution)/shard_map/ppermute | solution.py:104
  20.3 5.3 %collective-permute-start.3 = (bf16[3,16,1024]{2,1,0:T(8,128)(2,1)S(1)}, bf16[3,16,1024]{2,1,0:T(8,128)(2,1)S(1)}, u32[]{:S(2)}, u32[]{:S(2)}) collective-permute-start(bf16[3,16,1024]{2,1,0:T(8,128)(2,1)S(1)} %get-tuple-element.34), channel_id=1, source_target_pairs={{0,8},{8,0},{16,24},{24,16},{1,9},{9,1},{17,25},{25,17},{2,10},{10... | collective-permute-start | bytes 294920 | tf_op jit(solution)/shard_map/ppermute | solution.py:104
  20.3 5.6 %collective-permute-start.4 = (bf16[3,16,1024]{2,1,0:T(8,128)(2,1)S(1)}, bf16[3,16,1024]{2,1,0:T(8,128)(2,1)S(1)}, u32[]{:S(2)}, u32[]{:S(2)}) collective-permute-start(bf16[3,16,1024]{2,1,0:T(8,128)(2,1)S(1)} %get-tuple-element.35), channel_id=1, source_target_pairs={{0,16},{8,24},{16,0},{24,8},{1,17},{9,25},{17,1},{25,9},{2,18},{10... | collective-permute-start | bytes 294920 | tf_op jit(solution)/shard_map/ppermute | solution.py:104
  22.0 5.2 %collective-permute-start.5 = (bf16[3,16,1024]{2,1,0:T(8,128)(2,1)S(1)}, bf16[3,16,1024]{2,1,0:T(8,128)(2,1)S(1)}, u32[]{:S(2)}, u32[]{:S(2)}) collective-permute-start(bf16[3,16,1024]{2,1,0:T(8,128)(2,1)S(1)} %get-tuple-element.36), channel_id=1, source_target_pairs={{0,24},{8,16},{16,8},{24,0},{1,25},{9,17},{17,9},{25,1},{2,26},{10... | collective-permute-start | bytes 294920 | tf_op jit(solution)/shard_map/ppermute | solution.py:104
  27.5 5.0 %collective-permute-start.6 = (bf16[1,3,128,128]{3,2,1,0:T(8,128)(2,1)S(1)}, bf16[1,3,128,128]{3,2,1,0:T(8,128)(2,1)S(1)}, u32[]{:S(2)}, u32[]{:S(2)}) collective-permute-start(bf16[1,3,128,128]{3,2,1,0:T(8,128)(2,1)S(1)} %get-tuple-element.42), channel_id=1, source_target_pairs={{0,1},{1,0},{2,3},{3,2},{4,5},{5,4},{6,7},{7,6},{8,9},{9,8},{10,11... | collective-permute-start | bytes 294920 | tf_op jit(solution)/shard_map/ppermute | solution.py:104
  32.6 7.0 %collective-permute-start.9 = (bf16[1,3,128,128]{3,2,1,0:T(8,128)(2,1)S(1)}, bf16[1,3,128,128]{3,2,1,0:T(8,128)(2,1)S(1)}, u32[]{:S(2)}, u32[]{:S(2)}) collective-permute-start(bf16[1,3,128,128]{3,2,1,0:T(8,128)(2,1)S(1)} %add.3), channel_id=1, source_target_pairs={{0,6},{1,7},{2,0},{3,1},{4,2},{5,3},{6,4},{7,5},{8,14},{9,15},{10,... | collective-permute-start | bytes 294920 | tf_op jit(solution)/shard_map/ppermute | solution.py:104
  34.3 11.8 %collective-permute-start.8 = (bf16[1,3,128,128]{3,2,1,0:T(8,128)(2,1)S(1)}, bf16[1,3,128,128]{3,2,1,0:T(8,128)(2,1)S(1)}, u32[]{:S(2)}, u32[]{:S(2)}) collective-permute-start(bf16[1,3,128,128]{3,2,1,0:T(8,128)(2,1)S(1)} %add.3), channel_id=1, source_target_pairs={{0,4},{1,5},{2,6},{3,7},{4,0},{5,1},{6,2},{7,3},{8,12},{9,13},{10,... | collective-permute-start | bytes 294920 | tf_op jit(solution)/shard_map/ppermute | solution.py:104
  37.6 8.5 %collective-permute-start.7 = (bf16[1,3,128,128]{3,2,1,0:T(8,128)(2,1)S(1)}, bf16[1,3,128,128]{3,2,1,0:T(8,128)(2,1)S(1)}, u32[]{:S(2)}, u32[]{:S(2)}) collective-permute-start(bf16[1,3,128,128]{3,2,1,0:T(8,128)(2,1)S(1)} %add.3), channel_id=1, source_target_pairs={{0,2},{1,3},{2,4},{3,5},{4,6},{5,7},{6,0},{7,1},{8,10},{9,11},{10,... | collective-permute-start | bytes 294920 | tf_op jit(solution)/shard_map/ppermute | solution.py:104
  46.2 8.2 %collective-permute-start.11 = (bf16[4,3,128,128]{3,2,1,0:T(8,128)(2,1)S(1)}, bf16[4,3,128,128]{3,2,1,0:T(8,128)(2,1)S(1)}, u32[]{:S(2)}, u32[]{:S(2)}) collective-permute-start(bf16[4,3,128,128]{3,2,1,0:T(8,128)(2,1)S(1)} %pad_maximum_fusion.refs_0_), channel_id=1, source_target_pairs={{0,16},{8,24},{16,0},{24,8},{1,17},{9,25},{17,1},{25,9},{2,18},{10... | collective-permute-start | bytes 1179656 | tf_op jit(solution)/shard_map/ppermute | solution.py:104
  46.2 8.2 %collective-permute-start.10 = (bf16[4,3,128,128]{3,2,1,0:T(8,128)(2,1)S(1)}, bf16[4,3,128,128]{3,2,1,0:T(8,128)(2,1)S(1)}, u32[]{:S(2)}, u32[]{:S(2)}) collective-permute-start(bf16[4,3,128,128]{3,2,1,0:T(8,128)(2,1)S(1)} %pad_maximum_fusion.refs_0_), channel_id=1, source_target_pairs={{0,1},{1,0},{2,3},{3,2},{4,5},{5,4},{6,7},{7,6},{8,9},{9,8},{10,11... | collective-permute-start | bytes 1179656 | tf_op jit(solution)/shard_map/ppermute | solution.py:104
  51.5 6.7 %collective-permute-start.15 = (bf16[4,3,128,128]{3,2,1,0:T(8,128)(2,1)S(1)}, bf16[4,3,128,128]{3,2,1,0:T(8,128)(2,1)S(1)}, u32[]{:S(2)}, u32[]{:S(2)}) collective-permute-start(bf16[4,3,128,128]{3,2,1,0:T(8,128)(2,1)S(1)} %pad_maximum_fusion.refs_0_), channel_id=1, source_target_pairs={{0,8},{8,0},{16,24},{24,16},{1,9},{9,1},{17,25},{25,17},{2,10},{10... | collective-permute-start | bytes 1179656 | tf_op jit(solution)/shard_map/ppermute | solution.py:104
  54.5 3.8 %collective-permute-start.16 = (bf16[4,3,128,128]{3,2,1,0:T(8,128)(2,1)S(1)}, bf16[4,3,128,128]{3,2,1,0:T(8,128)(2,1)S(1)}, u32[]{:S(2)}, u32[]{:S(2)}) collective-permute-start(bf16[4,3,128,128]{3,2,1,0:T(8,128)(2,1)S(1)} %collective-permute-done.11.refs_2_), channel_id=1, source_target_pairs={{0,8},{8,0},{16,24},{24,16},{1,9},{9,1},{17,25},{25,17},{2,10},{10... | collective-permute-start | bytes 1179656 | tf_op jit(solution)/shard_map/ppermute | solution.py:104
  54.5 9.2 %copy-start = (bf16[1024,1024]{1,0:T(8,128)(2,1)S(1)}, bf16[1024,1024]{1,0:T(8,128)(2,1)}, u32[]{:S(2)}) copy-start(bf16[1024,1024]{1,0:T(8,128)(2,1)} %constant.5.clone.table_ref.refs_1_) | copy-start | bytes 6291460
  54.5 12.1 %collective-permute-start.12 = (bf16[4,3,128,128]{3,2,1,0:T(8,128)(2,1)S(1)}, bf16[4,3,128,128]{3,2,1,0:T(8,128)(2,1)S(1)}, u32[]{:S(2)}, u32[]{:S(2)}) collective-permute-start(bf16[4,3,128,128]{3,2,1,0:T(8,128)(2,1)S(1)} %collective-permute-done.10.refs_0_), channel_id=1, source_target_pairs={{0,8},{8,0},{16,24},{24,16},{1,9},{9,1},{17,25},{25,17},{2,10},{10... | collective-permute-start | bytes 1179656 | tf_op jit(solution)/shard_map/ppermute | solution.py:104
  55.1 6.9 %collective-permute-start.14 = (bf16[4,3,64,128]{3,2,1,0:T(8,128)(2,1)S(1)}, bf16[4,3,64,128]{3,2,1,0:T(8,128)(2,1)S(1)}, u32[]{:S(2)}, u32[]{:S(2)}) collective-permute-start(bf16[4,3,64,128]{3,2,1,0:T(8,128)(2,1)S(1)} %slice.7), channel_id=1, source_target_pairs={{0,1},{1,0},{2,3},{3,2},{4,5},{5,4},{6,7},{7,6},{8,9},{9,8},{10,11... | collective-permute-start | bytes 589832 | tf_op jit(solution)/shard_map/ppermute | solution.py:104
  56.6 6.6 %collective-permute-start.13 = (bf16[4,3,64,128]{3,2,1,0:T(8,128)(2,1)S(1)}, bf16[4,3,64,128]{3,2,1,0:T(8,128)(2,1)S(1)}, u32[]{:S(2)}, u32[]{:S(2)}) collective-permute-start(bf16[4,3,64,128]{3,2,1,0:T(8,128)(2,1)S(1)} %slice.6), channel_id=1, source_target_pairs={{0,16},{8,24},{16,0},{24,8},{1,17},{9,25},{17,1},{25,9},{2,18},{10... | collective-permute-start | bytes 589832 | tf_op jit(solution)/shard_map/ppermute | solution.py:104
  63.2 3.4 %collective-permute-start.17 = (bf16[4,3,64,128]{3,2,1,0:T(8,128)(2,1)S(1)}, bf16[4,3,64,128]{3,2,1,0:T(8,128)(2,1)S(1)}, u32[]{:S(2)}, u32[]{:S(2)}) collective-permute-start(bf16[4,3,64,128]{3,2,1,0:T(8,128)(2,1)S(1)} %collective-permute-done.13.refs_2_), channel_id=1, source_target_pairs={{0,8},{8,0},{16,24},{24,16},{1,9},{9,1},{17,25},{25,17},{2,10},{10... | collective-permute-start | bytes 589832 | tf_op jit(solution)/shard_map/ppermute | solution.py:104
  63.2 3.5 %collective-permute-start.18 = (bf16[4,3,64,128]{3,2,1,0:T(8,128)(2,1)S(1)}, bf16[4,3,64,128]{3,2,1,0:T(8,128)(2,1)S(1)}, u32[]{:S(2)}, u32[]{:S(2)}) collective-permute-start(bf16[4,3,64,128]{3,2,1,0:T(8,128)(2,1)S(1)} %collective-permute-done.14.refs_3_), channel_id=1, source_target_pairs={{0,8},{8,0},{16,24},{24,16},{1,9},{9,1},{17,25},{25,17},{2,10},{10... | collective-permute-start | bytes 589832 | tf_op jit(solution)/shard_map/ppermute | solution.py:104

commit v4 on v3

--- a/solution.py
+++ b/solution.py
@@ -127,7 +127,7 @@
     for w in range(windows):
         mine = pl.ds(w * chans, chans)
         fetches.append(pltpu.make_async_copy(x_hbm.at[mine], x_ref.at[mine], sems.at[w]))
-        fetches[-1].start()
+    fetches[0].start()
     fetch_fir.wait()
     filter_matrix(fir_ref[...].astype(jnp.float32), toeplitz)
     step = 4 * FIR_OUT
@@ -148,6 +148,8 @@
     for w in range(windows):
         mine = slice(w * chans, (w + 1) * chans)
         fetches[w].wait()
+        if w + 1 < windows:
+            fetches[w + 1].start()
         pieces = [jnp.concatenate([jnp.zeros((chans, 128), jnp.bfloat16), x_ref[mine, :step]], axis=1)]
         for n in range(1, together):
             pieces.append(x_ref[mine, n * step - 128 : (n + 1) * step])
@@ -519,9 +521,9 @@
     for y in range(sizes["y"]):
         if y > 0:
             far = {key: array for key, array in held.items() if key[0] and key[1]}
-            far, cross = lax.optimization_barrier((far, cross))
+            earlier.append(lag_parts(cross, sizes, y - 1))
+            far, earlier = lax.optimization_barrier((far, earlier))
             held.update(far)
-            earlier.append(lag_parts(cross, sizes, y - 1))
         arrays, fetch = rows_of(y)
         cross = crossed(expanded, arrays, fetch, sizes, by_y=y)
     return correlations(cross, earlier, window_total, sizes, sizes["y"] - 1)

time: 75 us -> 74.9 us (level)
  no operation moved by 1% of the time
where the time goes in v4:
time: 74.9 us; the launch traced here: 74.7 us
  Pallas kernels  25.7 us (34%)
  starting transfers between devices  23.3 us (31%)
  waiting for transfers between devices  19.3 us (26%)
  matrix products  5.33 us (7%)
    ppermute x19, starting transfers between devices, shifted(): return lax.ppermute(value, axis, pairs)  23.3 us
    ppermute x19, waiting for transfers between devices, shifted(): return lax.ppermute(value, axis, pairs)  19.3 us
    pallas_call x1, Pallas kernels, whitened_spectra(): pl.pallas_call(functools.partial(fir_kernel, windows=windows), in_specs=[...  6.33 us
    pallas_call x2, Pallas kernels, crossed(): pl.pallas_call(functools.partial(cross_kernel, fetch=fetch, own=own, size...  6.28 us
    dot_general x1, matrix products, dot(): return jnp.dot(a, b, preferred_element_type=jnp.float32)  5.33 us
    pallas_call x1, Pallas kernels, correlations(): pl.pallas_call(functools.partial(lag_kernel, scale=1.0 / math.sqrt(NFREQ...  4.8 us
    pallas_call x1, Pallas kernels, expanded_local(): pl.pallas_call(functools.partial(expand_kernel, sizes=sizes), out_shape=j...  3.71 us
    pallas_call x1, Pallas kernels, lag_parts(): pl.pallas_call(functools.partial(part_kernel, sizes=sizes, by_y=by_y), ou...  2.93 us
  transfers between devices with their start and end apart: 19, of which 10 were waited for; matrix products, arithmetic and copies ran while one was open for 0% of the time, Pallas kernels for 13%

profile of v4, /device:TPU:0, one launch (start us, length us, event | category | flops | bytes accessed | tf_op | source)
XLA Modules:
  0.0 74.7 jit_solution(14466812054929230887)
XLA Ops:
  0.7 6.3 %fir.1 = bf16[8,192,1536]{2,1,0:T(8,128)(2,1)S(1)} custom-call(bf16[192,16384]{1,0:T(8,128)(2,1)} %bitcast.14, bf16[1,32]{1,0:T(2,128)(2,1)S(1)} %bitcast.10), custom_call_target="tpu_custom_call" | custom-call | tf_op jit(solution)/shard_map/fir/pallas_call | solution.py:230
  7.0 5.3 %fusion.part_ref = f32[8,192,1024]{2,1,0:T(8,128)S(1)} fusion(bf16[8,192,1536]{2,1,0:T(8,128)(2,1)S(1)} %fir.1, bf16[1536,1024,1]{1,0,2:T(8,128)(2,1)S(1)} %copy-done.3), kind=kOutput, calls=%fused_computation.1 | convolution fusion | flops 4831838208 | bytes 14155776 | tf_op jit(solution)/shard_map/dot_general | solution.py:48
  12.4 1.3 %whiten.1 = (bf16[2,192,128]{2,1,0:T(8,128)(2,1)S(1)}, bf16[2,192,128]{2,1,0:T(8,128)(2,1)S(1)}, bf16[2,192,128]{2,1,0:T(8,128)(2,1)S(1)}, bf16[2,192,128]{2,1,0...) custom-call(f32[8,192,1024]{2,1,0:T(8,128)S(1)} %fusion.part_ref), custom_call_target="tpu_custom_call" | custom-call | tf_op jit(solution)/shard_map/whiten/pallas_call | solution.py:244
  13.7 3.1 %collective-permute-start = (bf16[2,192,128]{2,1,0:T(8,128)(2,1)S(1)}, bf16[2,192,128]{2,1,0:T(8,128)(2,1)S(1)}, u32[]{:S(2)}, u32[]{:S(2)}) collective-permute-start(bf16[2,192,128]{2,1,0:T(8,128)(2,1)S(1)} %get-tuple-element.30), channel_id=1, source_target_pairs={{0,2},{1,3},{2,4},{3,5},{4,6},{5,7},{6,0},{7,1},{8,10},{9,11},{10,... | collective-permute-start | bytes 294920 | tf_op jit(solution)/shard_map/ppermute | solution.py:104
  16.8 2.6 %collective-permute-start.1 = (bf16[2,192,128]{2,1,0:T(8,128)(2,1)S(1)}, bf16[2,192,128]{2,1,0:T(8,128)(2,1)S(1)}, u32[]{:S(2)}, u32[]{:S(2)}) collective-permute-start(bf16[2,192,128]{2,1,0:T(8,128)(2,1)S(1)} %get-tuple-element.31), channel_id=1, source_target_pairs={{0,4},{1,5},{2,6},{3,7},{4,0},{5,1},{6,2},{7,3},{8,12},{9,13},{10,... | collective-permute-start | bytes 294920 | tf_op jit(solution)/shard_map/ppermute | solution.py:104
  19.4 1.3 %collective-permute-start.2 = (bf16[2,192,128]{2,1,0:T(8,128)(2,1)S(1)}, bf16[2,192,128]{2,1,0:T(8,128)(2,1)S(1)}, u32[]{:S(2)}, u32[]{:S(2)}) collective-permute-start(bf16[2,192,128]{2,1,0:T(8,128)(2,1)S(1)} %get-tuple-element.32), channel_id=1, source_target_pairs={{0,6},{1,7},{2,0},{3,1},{4,2},{5,3},{6,4},{7,5},{8,14},{9,15},{10,... | collective-permute-start | bytes 294920 | tf_op jit(solution)/shard_map/ppermute | solution.py:104
  20.7 1.5 %collective-permute-start.4 = (bf16[3,16,1024]{2,1,0:T(8,128)(2,1)S(1)}, bf16[3,16,1024]{2,1,0:T(8,128)(2,1)S(1)}, u32[]{:S(2)}, u32[]{:S(2)}) collective-permute-start(bf16[3,16,1024]{2,1,0:T(8,128)(2,1)S(1)} %get-tuple-element.35), channel_id=1, source_target_pairs={{0,16},{8,24},{16,0},{24,8},{1,17},{9,25},{17,1},{25,9},{2,18},{10... | collective-permute-start | bytes 294920 | tf_op jit(solution)/shard_map/ppermute | solution.py:104
  22.6 3.4 %collective-permute-done.1.refs_2_ = bf16[2,192,128]{2,1,0:T(8,128)(2,1)S(1)} collective-permute-done((bf16[2,192,128]{2,1,0:T(8,128)(2,1)S(1)}, bf16[2,192,128]{2,1,0:T(8,128)(2,1)S(1)}, u32[]{:S(2)}, u32[]{:S(2)}) %collective-permute-start.1) | collective-permute-done | bytes 98336 | tf_op jit(solution)/shard_map/ppermute | solution.py:104
  26.3 1.3 %collective-permute-done.5.refs_3_ = bf16[3,16,1024]{2,1,0:T(8,128)(2,1)S(1)} collective-permute-done((bf16[3,16,1024]{2,1,0:T(8,128)(2,1)S(1)}, bf16[3,16,1024]{2,1,0:T(8,128)(2,1)S(1)}, u32[]{:S(2)}, u32[]{:S(2)}) %collective-permute-start.5) | collective-permute-done | bytes 98336 | tf_op jit(solution)/shard_map/ppermute | solution.py:104
  28.0 1.6 %collective-permute-start.6 = (bf16[1,3,128,128]{3,2,1,0:T(8,128)(2,1)S(1)}, bf16[1,3,128,128]{3,2,1,0:T(8,128)(2,1)S(1)}, u32[]{:S(2)}, u32[]{:S(2)}) collective-permute-start(bf16[1,3,128,128]{3,2,1,0:T(8,128)(2,1)S(1)} %get-tuple-element.42), channel_id=1, source_target_pairs={{0,1},{1,0},{2,3},{3,2},{4,5},{5,4},{6,7},{7,6},{8,9},{9,8},{10,11... | collective-permute-start | bytes 294920 | tf_op jit(solution)/shard_map/ppermute | solution.py:104
  29.6 3.4 %collective-permute-done.6 = bf16[1,3,128,128]{3,2,1,0:T(8,128)(2,1)S(1)} collective-permute-done((bf16[1,3,128,128]{3,2,1,0:T(8,128)(2,1)S(1)}, bf16[1,3,128,128]{3,2,1,0:T(8,128)(2,1)S(1)}, u32[]{:S(2)}, u32[]{:S(2)}) %collective-permute-start.6) | collective-permute-done | bytes 98336 | tf_op jit(solution)/shard_map/ppermute | solution.py:104
  33.0 1.7 %collective-permute-start.9 = (bf16[1,3,128,128]{3,2,1,0:T(8,128)(2,1)S(1)}, bf16[1,3,128,128]{3,2,1,0:T(8,128)(2,1)S(1)}, u32[]{:S(2)}, u32[]{:S(2)}) collective-permute-start(bf16[1,3,128,128]{3,2,1,0:T(8,128)(2,1)S(1)} %add.3), channel_id=1, source_target_pairs={{0,6},{1,7},{2,0},{3,1},{4,2},{5,3},{6,4},{7,5},{8,14},{9,15},{10,... | collective-permute-start | bytes 294920 | tf_op jit(solution)/shard_map/ppermute | solution.py:104
  34.7 3.3 %collective-permute-start.8 = (bf16[1,3,128,128]{3,2,1,0:T(8,128)(2,1)S(1)}, bf16[1,3,128,128]{3,2,1,0:T(8,128)(2,1)S(1)}, u32[]{:S(2)}, u32[]{:S(2)}) collective-permute-start(bf16[1,3,128,128]{3,2,1,0:T(8,128)(2,1)S(1)} %add.3), channel_id=1, source_target_pairs={{0,4},{1,5},{2,6},{3,7},{4,0},{5,1},{6,2},{7,3},{8,12},{9,13},{10,... | collective-permute-start | bytes 294920 | tf_op jit(solution)/shard_map/ppermute | solution.py:104
  38.1 1.9 %collective-permute-start.7 = (bf16[1,3,128,128]{3,2,1,0:T(8,128)(2,1)S(1)}, bf16[1,3,128,128]{3,2,1,0:T(8,128)(2,1)S(1)}, u32[]{:S(2)}, u32[]{:S(2)}) collective-permute-start(bf16[1,3,128,128]{3,2,1,0:T(8,128)(2,1)S(1)} %add.3), channel_id=1, source_target_pairs={{0,2},{1,3},{2,4},{3,5},{4,6},{5,7},{6,0},{7,1},{8,10},{9,11},{10,... | collective-permute-start | bytes 294920 | tf_op jit(solution)/shard_map/ppermute | solution.py:104
  40.0 6.5 %collective-permute-done.8 = bf16[1,3,128,128]{3,2,1,0:T(8,128)(2,1)S(1)} collective-permute-done((bf16[1,3,128,128]{3,2,1,0:T(8,128)(2,1)S(1)}, bf16[1,3,128,128]{3,2,1,0:T(8,128)(2,1)S(1)}, u32[]{:S(2)}, u32[]{:S(2)}) %collective-permute-start.8) | collective-permute-done | bytes 98336 | tf_op jit(solution)/shard_map/ppermute | solution.py:104
  46.7 1.6 %collective-permute-start.10 = (bf16[4,3,128,128]{3,2,1,0:T(8,128)(2,1)S(1)}, bf16[4,3,128,128]{3,2,1,0:T(8,128)(2,1)S(1)}, u32[]{:S(2)}, u32[]{:S(2)}) collective-permute-start(bf16[4,3,128,128]{3,2,1,0:T(8,128)(2,1)S(1)} %pad_maximum_fusion.refs_0_), channel_id=1, source_target_pairs={{0,1},{1,0},{2,3},{3,2},{4,5},{5,4},{6,7},{7,6},{8,9},{9,8},{10,11... | collective-permute-start | bytes 1179656 | tf_op jit(solution)/shard_map/ppermute | solution.py:104
  48.3 3.7 %expand.1 = bf16[64,16,16,192]{3,2,1,0:T(8,128)(2,1)S(1)} custom-call(bf16[3,16,1024]{2,1,0:T(8,128)(2,1)S(1)} %get-tuple-element.43.refs_0_, bf16[3,16,1024]{2,1,0:T(8,128)(2,1)S(1)} %collective-permute-done.3.refs_1_, bf16[3,16,1024]{2,1,0:T(8,128)(2,1)S(1)} %collective-permute-done.4.refs_2_, bf16[3,16,1024]{2,1,0:T(8,128)(2,1)S(1)} %collective-permute-done.5.refs_3_), custom_call_target="tpu_custom_call" | custom-call | flops 4000000000 | bytes 8388608 | tf_op jit(solution)/shard_map/expand/pallas_call | solution.py:335
  52.1 2.8 %collective-permute-done.11.refs_2_ = bf16[4,3,128,128]{3,2,1,0:T(8,128)(2,1)S(1)} collective-permute-done((bf16[4,3,128,128]{3,2,1,0:T(8,128)(2,1)S(1)}, bf16[4,3,128,128]{3,2,1,0:T(8,128)(2,1)S(1)}, u32[]{:S(2)}, u32[]{:S(2)}) %collective-permute-start.11) | collective-permute-done | bytes 393248 | tf_op jit(solution)/shard_map/ppermute | solution.py:104
  55.5 1.5 %collective-permute-start.14 = (bf16[4,3,64,128]{3,2,1,0:T(8,128)(2,1)S(1)}, bf16[4,3,64,128]{3,2,1,0:T(8,128)(2,1)S(1)}, u32[]{:S(2)}, u32[]{:S(2)}) collective-permute-start(bf16[4,3,64,128]{3,2,1,0:T(8,128)(2,1)S(1)} %slice.7), channel_id=1, source_target_pairs={{0,1},{1,0},{2,3},{3,2},{4,5},{5,4},{6,7},{7,6},{8,9},{9,8},{10,11... | collective-permute-start | bytes 589832 | tf_op jit(solution)/shard_map/ppermute | solution.py:104
  57.1 1.7 %collective-permute-start.13 = (bf16[4,3,64,128]{3,2,1,0:T(8,128)(2,1)S(1)}, bf16[4,3,64,128]{3,2,1,0:T(8,128)(2,1)S(1)}, u32[]{:S(2)}, u32[]{:S(2)}) collective-permute-start(bf16[4,3,64,128]{3,2,1,0:T(8,128)(2,1)S(1)} %slice.6), channel_id=1, source_target_pairs={{0,16},{8,24},{16,0},{24,8},{1,17},{9,25},{17,1},{25,9},{2,18},{10... | collective-permute-start | bytes 589832 | tf_op jit(solution)/shard_map/ppermute | solution.py:104
  58.7 3.1 %cross.2.cross_ref = bf16[2048,512]{1,0:T(8,128)(2,1)S(1)} custom-call(bf16[64,256,192]{2,1,0:T(8,128)(2,1)S(1)} %bitcast.12, bf16[4,3,128,128]{3,2,1,0:T(8,128)(2,1)S(1)} %pad_maximum_fusion.refs_0_, bf16[4,3,128,128]{3,2,1,0:T(8,128)(2,1)S(1)} %collective-permute-done.15.refs_1_, bf16[4,3,128,128]{3,2,1,0:T(8,128)(2,1)S(1)} %collective-permute-done.11.refs_2_, ...), custom_call_target="tpu_custom_call" | custom-call | flops 4000000000 | bytes 8388608 | tf_op jit(solution)/shard_map/cross/pallas_call | solution.py:380
  61.9 2.9 %lags_near.1.refs_2_ = f32[2048,1024]{1,0:T(8,128)S(1)} custom-call(bf16[2048,512]{1,0:T(8,128)(2,1)S(1)} %cross.2.cross_ref, bf16[1024,1024]{1,0:T(8,128)(2,1)S(1)} %copy-done), custom_call_target="tpu_custom_call" | custom-call | flops 4000000000 | bytes 8388608 | tf_op jit(solution)/shard_map/lags_near/pallas_call | solution.py:450
  66.6 3.1 %cross.3.refs_0_ = bf16[2048,512]{1,0:T(8,128)(2,1)S(1)} custom-call(bf16[64,256,192]{2,1,0:T(8,128)(2,1)S(1)} %bitcast.13, bf16[4,3,128,128]{3,2,1,0:T(8,128)(2,1)S(1)} %collective-permute-done.10.refs_0_, bf16[4,3,128,128]{3,2,1,0:T(8,128)(2,1)S(1)} %collective-permute-done.12.refs_1_, bf16[4,3,64,128]{3,2,1,0:T(8,128)(2,1)S(1)} %collective-permute-done.13.refs_2_, ...), custom_call_target="tpu_custom_call" | custom-call | flops 4000000000 | bytes 8388608 | tf_op jit(solution)/shard_map/cross/pallas_call | solution.py:380
  69.8 4.8 %lags.1 = f32[2048,1024]{1,0:T(8,128)} custom-call(bf16[2048,512]{1,0:T(8,128)(2,1)S(1)} %cross.3.refs_0_, bf16[1024,1024]{1,0:T(8,128)(2,1)S(1)} %copy-done, f32[2048,1024]{1,0:T(8,128)S(1)} %lags_near.1.refs_2_), custom_call_target="tpu_custom_call" | custom-call | tf_op jit(solution)/shard_map/lags/pallas_call | solution.py:463
  (35 shorter events, 4.4 us)
Async XLA Ops:
  0.0 0.7 copy-start.1
  0.7 6.3 %copy-start.3 = (bf16[1536,1024,1]{1,0,2:T(8,128)(2,1)S(1)}, bf16[1536,1024,1]{1,0,2:T(8,128)(2,1)}, u32[]{:S(2)}) copy-start(bf16[1536,1024,1]{1,0,2:T(8,128)(2,1)} %constant.7) | copy-start | bytes 9437188
  12.3 15.3 %copy-start.2 = (s32[128]{0:T(128)S(1)}, s32[128]{0:T(128)}, u32[]{:S(2)}) copy-start(s32[128]{0:T(128)} %param.8) | copy-start | bytes 1540
  13.7 8.7 %collective-permute-start = (bf16[2,192,128]{2,1,0:T(8,128)(2,1)S(1)}, bf16[2,192,128]{2,1,0:T(8,128)(2,1)S(1)}, u32[]{:S(2)}, u32[]{:S(2)}) collective-permute-start(bf16[2,192,128]{2,1,0:T(8,128)(2,1)S(1)} %get-tuple-element.30), channel_id=1, source_target_pairs={{0,2},{1,3},{2,4},{3,5},{4,6},{5,7},{6,0},{7,1},{8,10},{9,11},{10,... | collective-permute-start | bytes 294920 | tf_op jit(solution)/shard_map/ppermute | solution.py:104
  16.8 9.2 %collective-permute-start.1 = (bf16[2,192,128]{2,1,0:T(8,128)(2,1)S(1)}, bf16[2,192,128]{2,1,0:T(8,128)(2,1)S(1)}, u32[]{:S(2)}, u32[]{:S(2)}) collective-permute-start(bf16[2,192,128]{2,1,0:T(8,128)(2,1)S(1)} %get-tuple-element.31), channel_id=1, source_target_pairs={{0,4},{1,5},{2,6},{3,7},{4,0},{5,1},{6,2},{7,3},{8,12},{9,13},{10,... | collective-permute-start | bytes 294920 | tf_op jit(solution)/shard_map/ppermute | solution.py:104
  19.4 6.6 %collective-permute-start.2 = (bf16[2,192,128]{2,1,0:T(8,128)(2,1)S(1)}, bf16[2,192,128]{2,1,0:T(8,128)(2,1)S(1)}, u32[]{:S(2)}, u32[]{:S(2)}) collective-permute-start(bf16[2,192,128]{2,1,0:T(8,128)(2,1)S(1)} %get-tuple-element.32), channel_id=1, source_target_pairs={{0,6},{1,7},{2,0},{3,1},{4,2},{5,3},{6,4},{7,5},{8,14},{9,15},{10,... | collective-permute-start | bytes 294920 | tf_op jit(solution)/shard_map/ppermute | solution.py:104
  20.7 5.3 %collective-permute-start.3 = (bf16[3,16,1024]{2,1,0:T(8,128)(2,1)S(1)}, bf16[3,16,1024]{2,1,0:T(8,128)(2,1)S(1)}, u32[]{:S(2)}, u32[]{:S(2)}) collective-permute-start(bf16[3,16,1024]{2,1,0:T(8,128)(2,1)S(1)} %get-tuple-element.34), channel_id=1, source_target_pairs={{0,8},{8,0},{16,24},{24,16},{1,9},{9,1},{17,25},{25,17},{2,10},{10... | collective-permute-start | bytes 294920 | tf_op jit(solution)/shard_map/ppermute | solution.py:104
  20.7 5.6 %collective-permute-start.4 = (bf16[3,16,1024]{2,1,0:T(8,128)(2,1)S(1)}, bf16[3,16,1024]{2,1,0:T(8,128)(2,1)S(1)}, u32[]{:S(2)}, u32[]{:S(2)}) collective-permute-start(bf16[3,16,1024]{2,1,0:T(8,128)(2,1)S(1)} %get-tuple-element.35), channel_id=1, source_target_pairs={{0,16},{8,24},{16,0},{24,8},{1,17},{9,25},{17,1},{25,9},{2,18},{10... | collective-permute-start | bytes 294920 | tf_op jit(solution)/shard_map/ppermute | solution.py:104
  22.5 5.2 %collective-permute-start.5 = (bf16[3,16,1024]{2,1,0:T(8,128)(2,1)S(1)}, bf16[3,16,1024]{2,1,0:T(8,128)(2,1)S(1)}, u32[]{:S(2)}, u32[]{:S(2)}) collective-permute-start(bf16[3,16,1024]{2,1,0:T(8,128)(2,1)S(1)} %get-tuple-element.36), channel_id=1, source_target_pairs={{0,24},{8,16},{16,8},{24,0},{1,25},{9,17},{17,9},{25,1},{2,26},{10... | collective-permute-start | bytes 294920 | tf_op jit(solution)/shard_map/ppermute | solution.py:104
  28.0 5.0 %collective-permute-start.6 = (bf16[1,3,128,128]{3,2,1,0:T(8,128)(2,1)S(1)}, bf16[1,3,128,128]{3,2,1,0:T(8,128)(2,1)S(1)}, u32[]{:S(2)}, u32[]{:S(2)}) collective-permute-start(bf16[1,3,128,128]{3,2,1,0:T(8,128)(2,1)S(1)} %get-tuple-element.42), channel_id=1, source_target_pairs={{0,1},{1,0},{2,3},{3,2},{4,5},{5,4},{6,7},{7,6},{8,9},{9,8},{10,11... | collective-permute-start | bytes 294920 | tf_op jit(solution)/shard_map/ppermute | solution.py:104
  33.0 7.0 %collective-permute-start.9 = (bf16[1,3,128,128]{3,2,1,0:T(8,128)(2,1)S(1)}, bf16[1,3,128,128]{3,2,1,0:T(8,128)(2,1)S(1)}, u32[]{:S(2)}, u32[]{:S(2)}) collective-permute-start(bf16[1,3,128,128]{3,2,1,0:T(8,128)(2,1)S(1)} %add.3), channel_id=1, source_target_pairs={{0,6},{1,7},{2,0},{3,1},{4,2},{5,3},{6,4},{7,5},{8,14},{9,15},{10,... | collective-permute-start | bytes 294920 | tf_op jit(solution)/shard_map/ppermute | solution.py:104
  34.7 11.8 %collective-permute-start.8 = (bf16[1,3,128,128]{3,2,1,0:T(8,128)(2,1)S(1)}, bf16[1,3,128,128]{3,2,1,0:T(8,128)(2,1)S(1)}, u32[]{:S(2)}, u32[]{:S(2)}) collective-permute-start(bf16[1,3,128,128]{3,2,1,0:T(8,128)(2,1)S(1)} %add.3), channel_id=1, source_target_pairs={{0,4},{1,5},{2,6},{3,7},{4,0},{5,1},{6,2},{7,3},{8,12},{9,13},{10,... | collective-permute-start | bytes 294920 | tf_op jit(solution)/shard_map/ppermute | solution.py:104
  38.1 8.5 %collective-permute-start.7 = (bf16[1,3,128,128]{3,2,1,0:T(8,128)(2,1)S(1)}, bf16[1,3,128,128]{3,2,1,0:T(8,128)(2,1)S(1)}, u32[]{:S(2)}, u32[]{:S(2)}) collective-permute-start(bf16[1,3,128,128]{3,2,1,0:T(8,128)(2,1)S(1)} %add.3), channel_id=1, source_target_pairs={{0,2},{1,3},{2,4},{3,5},{4,6},{5,7},{6,0},{7,1},{8,10},{9,11},{10,... | collective-permute-start | bytes 294920 | tf_op jit(solution)/shard_map/ppermute | solution.py:104
  46.6 8.2 %collective-permute-start.11 = (bf16[4,3,128,128]{3,2,1,0:T(8,128)(2,1)S(1)}, bf16[4,3,128,128]{3,2,1,0:T(8,128)(2,1)S(1)}, u32[]{:S(2)}, u32[]{:S(2)}) collective-permute-start(bf16[4,3,128,128]{3,2,1,0:T(8,128)(2,1)S(1)} %pad_maximum_fusion.refs_0_), channel_id=1, source_target_pairs={{0,16},{8,24},{16,0},{24,8},{1,17},{9,25},{17,1},{25,9},{2,18},{10... | collective-permute-start | bytes 1179656 | tf_op jit(solution)/shard_map/ppermute | solution.py:104
  46.7 8.2 %collective-permute-start.10 = (bf16[4,3,128,128]{3,2,1,0:T(8,128)(2,1)S(1)}, bf16[4,3,128,128]{3,2,1,0:T(8,128)(2,1)S(1)}, u32[]{:S(2)}, u32[]{:S(2)}) collective-permute-start(bf16[4,3,128,128]{3,2,1,0:T(8,128)(2,1)S(1)} %pad_maximum_fusion.refs_0_), channel_id=1, source_target_pairs={{0,1},{1,0},{2,3},{3,2},{4,5},{5,4},{6,7},{7,6},{8,9},{9,8},{10,11... | collective-permute-start | bytes 1179656 | tf_op jit(solution)/shard_map/ppermute | solution.py:104
  52.0 6.7 %collective-permute-start.15 = (bf16[4,3,128,128]{3,2,1,0:T(8,128)(2,1)S(1)}, bf16[4,3,128,128]{3,2,1,0:T(8,128)(2,1)S(1)}, u32[]{:S(2)}, u32[]{:S(2)}) collective-permute-start(bf16[4,3,128,128]{3,2,1,0:T(8,128)(2,1)S(1)} %pad_maximum_fusion.refs_0_), channel_id=1, source_target_pairs={{0,8},{8,0},{16,24},{24,16},{1,9},{9,1},{17,25},{25,17},{2,10},{10... | collective-permute-start | bytes 1179656 | tf_op jit(solution)/shard_map/ppermute | solution.py:104
  54.9 3.8 %collective-permute-start.16 = (bf16[4,3,128,128]{3,2,1,0:T(8,128)(2,1)S(1)}, bf16[4,3,128,128]{3,2,1,0:T(8,128)(2,1)S(1)}, u32[]{:S(2)}, u32[]{:S(2)}) collective-permute-start(bf16[4,3,128,128]{3,2,1,0:T(8,128)(2,1)S(1)} %collective-permute-done.11.refs_2_), channel_id=1, source_target_pairs={{0,8},{8,0},{16,24},{24,16},{1,9},{9,1},{17,25},{25,17},{2,10},{10... | collective-permute-start | bytes 1179656 | tf_op jit(solution)/shard_map/ppermute | solution.py:104
  54.9 6.9 %copy-start = (bf16[1024,1024]{1,0:T(8,128)(2,1)S(1)}, bf16[1024,1024]{1,0:T(8,128)(2,1)}, u32[]{:S(2)}) copy-start(bf16[1024,1024]{1,0:T(8,128)(2,1)} %constant.5.clone.table_ref.refs_1_) | copy-start | bytes 6291460
  55.0 10.5 %collective-permute-start.12 = (bf16[4,3,128,128]{3,2,1,0:T(8,128)(2,1)S(1)}, bf16[4,3,128,128]{3,2,1,0:T(8,128)(2,1)S(1)}, u32[]{:S(2)}, u32[]{:S(2)}) collective-permute-start(bf16[4,3,128,128]{3,2,1,0:T(8,128)(2,1)S(1)} %collective-permute-done.10.refs_0_), channel_id=1, source_target_pairs={{0,8},{8,0},{16,24},{24,16},{1,9},{9,1},{17,25},{25,17},{2,10},{10... | collective-permute-start | bytes 1179656 | tf_op jit(solution)/shard_map/ppermute | solution.py:104
  55.5 9.3 %collective-permute-start.14 = (bf16[4,3,64,128]{3,2,1,0:T(8,128)(2,1)S(1)}, bf16[4,3,64,128]{3,2,1,0:T(8,128)(2,1)S(1)}, u32[]{:S(2)}, u32[]{:S(2)}) collective-permute-start(bf16[4,3,64,128]{3,2,1,0:T(8,128)(2,1)S(1)} %slice.7), channel_id=1, source_target_pairs={{0,1},{1,0},{2,3},{3,2},{4,5},{5,4},{6,7},{7,6},{8,9},{9,8},{10,11... | collective-permute-start | bytes 589832 | tf_op jit(solution)/shard_map/ppermute | solution.py:104
  57.1 7.8 %collective-permute-start.13 = (bf16[4,3,64,128]{3,2,1,0:T(8,128)(2,1)S(1)}, bf16[4,3,64,128]{3,2,1,0:T(8,128)(2,1)S(1)}, u32[]{:S(2)}, u32[]{:S(2)}) collective-permute-start(bf16[4,3,64,128]{3,2,1,0:T(8,128)(2,1)S(1)} %slice.6), channel_id=1, source_target_pairs={{0,16},{8,24},{16,0},{24,8},{1,17},{9,25},{17,1},{25,9},{2,18},{10... | collective-permute-start | bytes 589832 | tf_op jit(solution)/shard_map/ppermute | solution.py:104
  64.8 1.5 %collective-permute-start.17 = (bf16[4,3,64,128]{3,2,1,0:T(8,128)(2,1)S(1)}, bf16[4,3,64,128]{3,2,1,0:T(8,128)(2,1)S(1)}, u32[]{:S(2)}, u32[]{:S(2)}) collective-permute-start(bf16[4,3,64,128]{3,2,1,0:T(8,128)(2,1)S(1)} %collective-permute-done.13.refs_2_), channel_id=1, source_target_pairs={{0,8},{8,0},{16,24},{24,16},{1,9},{9,1},{17,25},{25,17},{2,10},{10... | collective-permute-start | bytes 589832 | tf_op jit(solution)/shard_map/ppermute | solution.py:104
  64.9 1.7 %collective-permute-start.18 = (bf16[4,3,64,128]{3,2,1,0:T(8,128)(2,1)S(1)}, bf16[4,3,64,128]{3,2,1,0:T(8,128)(2,1)S(1)}, u32[]{:S(2)}, u32[]{:S(2)}) collective-permute-start(bf16[4,3,64,128]{3,2,1,0:T(8,128)(2,1)S(1)} %collective-permute-done.14.refs_3_), channel_id=1, source_target_pairs={{0,8},{8,0},{16,24},{24,16},{1,9},{9,1},{17,25},{25,17},{2,10},{10... | collective-permute-start | bytes 589832 | tf_op jit(solution)/shard_map/ppermute | solution.py:104
